TPU v7x, 256 devices: a whole 4x4x8 slice. The times are simulated.
256 devices in a mesh: front: 4 (over z_hi, core), row: 4 (over x), col: 16 (over y, z_lo).
Axes of the slice: x: 4, y: 4, z: 8 (z_hi: 2, z_lo: 4; z = z_hi * 4 + z_lo), core: 2. Of those that a mesh axis runs over, the one named last changes fastest.
Arguments:
- front_matrix: float32 [4, 4096, 4096], P('front', 'row', 'col'), may hold values from -1 to 6, as said below
- child_updates: float32 [4, 2, 2048, 2048], P('front', None, 'row', 'col'), may hold values from -2 to 1, as said below
- child_map: int32 [4, 2, 2048], P('front'), may hold values from 0 to 4095, as said below
Outputs:
- front_out: float32 [4, 4096, 4096], P('front', 'row', 'col')
Inputs may be any that keep to these rules, and one draw needn't show every extreme that they name: `front_matrix`: each front's matrix is symmetric; once both of its children's update blocks are added, the front is positive definite with no eigenvalue under 0.5. `child_updates`: each update block is symmetric and negative semidefinite. `child_map`: the entries of one child's map are distinct. Each aligned block of 128 entries has at most 16 values in any aligned block of 256 parent indices and exactly 16 in some; each aligned block of 512 entries has at most 128 values in any aligned block of 1024 parent indices and exactly 128 in some. For whichever of the two blockings has fewer blocks, every such count equals its bound. Each aligned block of 256 parent indices receives exactly 128 entries of one child, and each aligned block of 1024 exactly 512.
All inputs are finite; a program needn't handle non-finite values.
Results may differ from a plain program's by a relative error of at most 0.0001.
Values sent between devices are 32-bit elements; how exact they have to be, the bound alone decides.
A program may use at most 64 MiB of HBM per device.

v0:
```python
import jax
import jax.numpy as jnp
from jax import lax
from jax.sharding import PartitionSpec as P

PW = 256
ELIMINATED_COLS = 256


def from_partner(value, axis, bit):
    mask = 2**bit
    pairs = [(source, source ^ mask) for source in range(lax.axis_size(axis))]
    return lax.ppermute(value, axis, pairs)


def spread(block, axis, source):
    block = jnp.where(lax.axis_index(axis) == source, block, jnp.zeros_like(block))
    return lax.psum(block, axis)


def slot_plan(targets, shards, width, capacity):
    count = targets.shape[0]
    owner_shard = targets // width
    local_place = targets % width
    hit_table = (owner_shard[:, None] == jnp.arange(shards, dtype=jnp.int32)[None, :]).astype(
        jnp.int32
    )
    rank_table = jnp.cumsum(hit_table, axis=0) - 1
    rank_in_shard = jnp.sum(rank_table * hit_table, axis=1)
    slot_index = owner_shard * capacity + rank_in_shard
    source = (
        jnp.full((shards * capacity,), count, jnp.int32)
        .at[slot_index]
        .set(jnp.arange(count, dtype=jnp.int32))
    )
    ident = jnp.full((shards * capacity,), width, jnp.int32).at[slot_index].set(local_place)
    return (source, ident)


def place_ids(ident, width):
    count = ident.shape[0]
    return (
        jnp.full((width,), count, jnp.int32)
        .at[ident]
        .set(jnp.arange(count, dtype=jnp.int32), mode="drop")
    )


def pick_rows(front_entries, index):
    return jnp.take(front_entries, index, axis=0, mode="fill", fill_value=0.0)


def pick_columns(front_entries, index):
    return jnp.take(front_entries, index, axis=1, mode="fill", fill_value=0.0)


def extend_add(front_local, updates, child_maps):
    row_count = lax.axis_size("row")
    col_count = lax.axis_size("col")
    row_index = lax.axis_index("row")
    col_index = lax.axis_index("col")
    rows_child, cols_child = updates[0].shape
    rows_parent, cols_parent = front_local.shape
    child_order = child_maps[0].shape[0]
    cap_rows = child_order * (1 + min(1, row_count // (2 * col_count))) // row_count**2
    cap_cols = child_order * (1 + min(1, col_count // (2 * row_count))) // col_count**2
    row_plans = [
        slot_plan(
            lax.dynamic_slice_in_dim(mapping, row_index * rows_child, rows_child),
            row_count,
            rows_parent,
            cap_rows,
        )
        for mapping in child_maps
    ]
    col_plans = [
        slot_plan(
            lax.dynamic_slice_in_dim(mapping, col_index * cols_child, cols_child),
            col_count,
            cols_parent,
            cap_cols,
        )
        for mapping in child_maps
    ]
    packed = [pick_rows(updates[member], row_plans[member][0]) for member in range(2)]
    received = (
        lax.all_to_all(packed[0], "row", split_axis=0, concat_axis=0, tiled=True),
        lax.all_to_all(packed[1], "row", split_axis=0, concat_axis=0, tiled=True),
        lax.all_to_all(row_plans[0][1], "row", split_axis=0, concat_axis=0, tiled=True),
        lax.all_to_all(row_plans[1][1], "row", split_axis=0, concat_axis=0, tiled=True),
    )
    middle = [
        pick_rows(received[member], place_ids(received[member + 2], rows_parent))
        for member in range(2)
    ]
    packed_cols = [pick_columns(middle[member], col_plans[member][0]) for member in range(2)]
    received_cols = (
        lax.all_to_all(packed_cols[0], "col", split_axis=1, concat_axis=1, tiled=True),
        lax.all_to_all(packed_cols[1], "col", split_axis=1, concat_axis=1, tiled=True),
        lax.all_to_all(col_plans[0][1][None, :], "col", split_axis=1, concat_axis=1, tiled=True),
        lax.all_to_all(col_plans[1][1][None, :], "col", split_axis=1, concat_axis=1, tiled=True),
    )
    contributions = [
        pick_columns(received_cols[member], place_ids(received_cols[member + 2][0], cols_parent))
        for member in range(2)
    ]
    return front_local + contributions[0] + contributions[1]


def embed_factor(solved, factor, global_index, first_column):
    solved = jnp.where(global_index[:, None] < first_column, 0.0, solved)
    in_panel = (global_index >= first_column) & (global_index < first_column + PW)
    factor_rows = jnp.take(factor, jnp.clip(global_index - first_column, 0, PW - 1), axis=0)
    return jnp.where(in_panel[:, None], factor_rows, solved)


def per_device(front_matrix, child_updates, child_map):
    partner = from_partner((child_updates[0, 1], child_map[0, 1]), "front", 0)
    front_local = extend_add(
        front_matrix[0], (child_updates[0, 0], partner[0]), (child_map[0, 0], partner[1])
    )
    rows_parent, cols_parent = front_local.shape
    row_index = lax.axis_index("row")
    col_index = lax.axis_index("col")
    global_row_ids = row_index * rows_parent + jnp.arange(rows_parent, dtype=jnp.int32)
    global_column_ids = col_index * cols_parent + jnp.arange(cols_parent, dtype=jnp.int32)
    owner_col, col_offset = divmod(0, cols_parent)
    owner_row, row_offset = divmod(0, rows_parent)
    pivot_piece = front_local[row_offset : row_offset + PW, col_offset : col_offset + PW]
    pivot = spread(pivot_piece, "row", owner_row)
    factor = jnp.linalg.cholesky(pivot)
    column_part = front_local
    solved = jax.scipy.linalg.solve_triangular(factor, column_part.T, lower=True).T
    solved = embed_factor(solved, factor, global_row_ids, 0)
    left_factor = spread(solved, "col", owner_col)
    target_rows = global_column_ids - row_index * rows_parent
    in_range = (target_rows >= 0) & (target_rows < rows_parent)
    picked = jnp.take(left_factor, jnp.clip(target_rows, 0, rows_parent - 1), axis=0)
    masked_part = jnp.where(in_range[:, None], picked, 0.0)
    right_factor = lax.psum(masked_part, "row")
    front_local = front_local - lax.dot_general(
        left_factor,
        right_factor,
        (((1,), (1,)), ((), ())),
        precision=lax.Precision.HIGHEST,
        preferred_element_type=jnp.float32,
    )
    stored_factor = (col_offset, owner_col, left_factor)
    factored_front = front_local
    col_offset, owner_col, left_factor = stored_factor
    current = factored_front
    factored_front = factored_front.at[:, col_offset : col_offset + PW].set(
        jnp.where(col_index == owner_col, left_factor, current)
    )
    zeroed_mask = (global_row_ids[:, None] < ELIMINATED_COLS) & (
        global_column_ids[None, :] >= ELIMINATED_COLS
    )
    factored_front = jnp.where(zeroed_mask, 0.0, factored_front)
    return factored_front[None]


def solution(mesh):
    in_specs = (P("front", "row", "col"), P("front", None, "row", "col"), P("front", None, None))
    out_specs = P("front", "row", "col")
    return jax.shard_map(
        per_device, mesh=mesh, in_specs=in_specs, out_specs=out_specs, check_vma=False
    )
```

profile of v0, /device:TPU:8, one launch (start us, length us, event | category | flops | bytes accessed | tf_op | source)
XLA Modules:
  0.0 491.1 jit_solution(2257505140755373797)
XLA Ops:
  9.2 3.0 scatter_custom_fusion.1
  12.2 4.3 all-to-all-start.1
  25.7 4.8 all-to-all-start
  38.0 9.0 %all-to-all-start.3 = ((s32[1,16,16]{2,0,1:T(1,128)}), s32[1,16,16]{2,0,1:T(1,128)S(1)}, u32[]{:S(2)}, u32[]{:S(2)}) async-start(s32[1,16,16]{2,0,1:T(1,128)} %all_to_all.69), calls=%async_computation.3 | async-start | bytes 16384 | tf_op jit(solution)/shard_map/all_to_all | solution.py:100
  48.6 3.0 scatter_custom_fusion.7
  54.5 4.8 all-to-all-start.5
  64.5 7.5 %all-to-all-start.7 = ((s32[1,16,16]{2,0,1:T(1,128)}), s32[1,16,16]{2,0,1:T(1,128)S(1)}, u32[]{:S(2)}, u32[]{:S(2)}) async-start(s32[1,16,16]{2,0,1:T(1,128)} %all_to_all.80), calls=%async_computation.7 | async-start | bytes 16384 | tf_op jit(solution)/shard_map/all_to_all | solution.py:101
  72.9 5.6 %all-to-all-done.7 = s32[1,16,16]{2,0,1:T(1,128)S(1)} async-done(((s32[1,16,16]{2,0,1:T(1,128)}), s32[1,16,16]{2,0,1:T(1,128)S(1)}, u32[]{:S(2)}, u32[]{:S(2)}) %all-to-all-start.7) | async-done | bytes 1056 | tf_op jit(solution)/shard_map/all_to_all | solution.py:101
  78.5 3.4 all-to-all-start.4
  83.0 5.5 %all-to-all-done.4 = f32[4,128,128]{2,1,0:T(8,128)S(1)} async-done(((f32[4,128,128]{2,1,0:T(8,128)}), f32[4,128,128]{2,1,0:T(8,128)S(1)}, u32[]{:S(2)}, u32[]{:S(2)}) %all-to-all-start.4) | async-done | bytes 262176 | tf_op jit(solution)/shard_map/all_to_all | solution.py:88
  88.5 5.4 %all-to-all-start.2 = ((f32[1024,16,16]{0,2,1:T(8,128)}), f32[1024,16,16]{0,2,1:T(8,128)S(1)}, u32[]{:S(2)}, u32[]{:S(2)}) async-start(f32[1024,16,16]{0,2,1:T(8,128)} %bitcast.19), calls=%async_computation.2 | async-start | bytes 2097152 | tf_op jit(solution)/shard_map/all_to_all | solution.py:98
  97.5 2.8 gather_fusion.7
  102.9 11.4 %all-to-all-done.2 = f32[1024,16,16]{0,2,1:T(8,128)S(1)} async-done(((f32[1024,16,16]{0,2,1:T(8,128)}), f32[1024,16,16]{0,2,1:T(8,128)S(1)}, u32[]{:S(2)}, u32[]{:S(2)}) %all-to-all-start.2) | async-done | bytes 1048608 | tf_op jit(solution)/shard_map/all_to_all | solution.py:98
  114.3 6.3 %all-to-all-start.6 = ((f32[1024,16,16]{0,2,1:T(8,128)}), f32[1024,16,16]{0,2,1:T(8,128)S(1)}, u32[]{:S(2)}, u32[]{:S(2)}) async-start(f32[1024,16,16]{0,2,1:T(8,128)} %bitcast.33), calls=%async_computation.6 | async-start | bytes 2097152 | tf_op jit(solution)/shard_map/all_to_all | solution.py:99
  127.9 15.7 %all-to-all-done.6 = f32[1024,16,16]{0,2,1:T(8,128)S(1)} async-done(((f32[1024,16,16]{0,2,1:T(8,128)}), f32[1024,16,16]{0,2,1:T(8,128)S(1)}, u32[]{:S(2)}, u32[]{:S(2)}) %all-to-all-start.6) | async-done | bytes 1048608 | tf_op jit(solution)/shard_map/all_to_all | solution.py:99
  148.4 44.9 %all-reduce.5.cloned.1.call-done = f32[256,256]{0,1:T(8,128)} async-done(((f32[256,256]{0,1:T(8,128)}), f32[256,256]{0,1:T(8,128)}) %all-reduce.5.cloned.1.call-update) | async-done | bytes 262160 | tf_op jit(solution)/shard_map/psum | solution.py:18
  194.5 11.7 %cholesky.49 = f32[128,128]{1,0:T(8,128)S(1)} custom-call(f32[128,128]{1,0:T(8,128)S(1)} %cholesky.115), custom_call_target="Cholesky" | custom-call | tf_op jit(solution)/shard_map/jit(cholesky)/cholesky | solution.py:131
  206.3 9.8 %custom-call.15 = f32[1,128,128]{1,2,0:T(8,128)S(1)} custom-call(f32[1,128,128]{2,1,0:T(8,128)S(1)} %get-tuple-element.68), custom_call_target="InvertDiagBlocksLowerTriangular" | custom-call | tf_op jit(solution)/shard_map/jit(cholesky)/cholesky | solution.py:131
  216.6 11.7 %cholesky.103 = f32[128,128]{1,0:T(8,128)S(1)} custom-call(f32[128,128]{1,0:T(8,128)S(1)} %convolution_subtract_fusion.2), custom_call_target="Cholesky" | custom-call | tf_op jit(solution)/shard_map/jit(cholesky)/cholesky | solution.py:131
  232.3 3.7 gather_fusion
  236.3 6.0 %while.3 = (s32[]{:T(128)}, f32[256,256]{0,1:T(8,128)}, s32[2,2]{1,0:T(2,128)S(1)}, f32[2,128,128]{2,1,0:T(8,128)S(1)}, s32[]{:T(128)}) while((s32[]{:T(128)}, f32[256,256]{0,1:T(8,128)}, s32[2,2]{1,0:T(2,128)S(1)}, f32[2,128,128]{2,1,0:T(8,128)S(1)}, s32[]{:T(128)}) %tuple.44), condition=%wide.while_cond.1, body=%wide.while_body.1.sunk | while | flops 2 | bytes 393321 | solution.py:133
  242.4 19.7 %custom-call.16 = f32[2,128,128]{1,2,0:T(8,128)S(1)} custom-call(f32[2,128,128]{2,1,0:T(8,128)S(1)} %get-tuple-element.36), custom_call_target="InvertDiagBlocksLowerTriangular" | custom-call | tf_op jit(solution)/shard_map/jit(_solve_triangular)/triangular_solve | solution.py:133
  266.2 160.3 %all-reduce.7.cloned.1.call-done = f32[1024,256]{0,1:T(8,128)} async-done(((f32[1024,256]{0,1:T(8,128)}), f32[1024,256]{0,1:T(8,128)}) %all-reduce.7.cloned.1.call-update) | async-done | bytes 1048592 | tf_op jit(solution)/shard_map/psum | solution.py:18
  429.9 51.0 %all-reduce.9.cloned.1.call-done = f32[256,256]{0,1:T(8,128)} async-done(((f32[256,256]{0,1:T(8,128)}), f32[256,256]{0,1:T(8,128)}) %all-reduce.9.cloned.1.call-update) | async-done | bytes 262160 | tf_op jit(solution)/shard_map/psum | solution.py:140
  (170 shorter events, 70.2 us)
Async XLA Ops:
  12.2 13.5 %all-to-all-start.1 = ((s32[4,128,1]{1,2,0:T(1,128)}), s32[4,128,1]{1,2,0:T(1,128)S(1)}, u32[]{:S(2)}, u32[]{:S(2)}) async-start(s32[4,128,1]{1,2,0:T(1,128)} %bitcast.12), calls=%async_computation.1 | async-start | bytes 4096 | tf_op jit(solution)/shard_map/all_to_all | solution.py:89
  16.5 16.5 %collective-permute-start.1 = (s32[2048]{0:T(1024)S(1)}, s32[2048]{0:T(1024)S(1)}, u32[]{:S(2)}, u32[]{:S(2)}) collective-permute-start(s32[2048]{0:T(1024)S(1)} %bitcast.165), channel_id=1, source_target_pairs={{0,64},{64,0},{128,192},{192,128},{1,65},{65,1},{129,193},{193,129... | collective-permute-start | bytes 24584 | tf_op jit(solution)/shard_map/ppermute | solution.py:13
  17.5 43.2 %collective-permute-start = (f32[512,128]{1,0:T(8,128)S(1)}, f32[512,128]{1,0:T(8,128)S(1)}, u32[]{:S(2)}, u32[]{:S(2)}) collective-permute-start(f32[512,128]{1,0:T(8,128)S(1)} %get-tuple-element.66), channel_id=1, source_target_pairs={{0,64},{64,0},{128,192},{192,128},{1,65},{65,1},{129,193},{193,129... | collective-permute-start | bytes 786440 | tf_op jit(solution)/shard_map/ppermute | solution.py:13
  25.7 12.2 %all-to-all-start = ((f32[4,128,128]{2,1,0:T(8,128)}), f32[4,128,128]{2,1,0:T(8,128)S(1)}, u32[]{:S(2)}, u32[]{:S(2)}) async-start(f32[4,128,128]{2,1,0:T(8,128)} %bitcast.16), calls=%async_computation | async-start | bytes 524288 | tf_op jit(solution)/shard_map/all_to_all | solution.py:87
  38.0 16.5 %all-to-all-start.3 = ((s32[1,16,16]{2,0,1:T(1,128)}), s32[1,16,16]{2,0,1:T(1,128)S(1)}, u32[]{:S(2)}, u32[]{:S(2)}) async-start(s32[1,16,16]{2,0,1:T(1,128)} %all_to_all.69), calls=%async_computation.3 | async-start | bytes 16384 | tf_op jit(solution)/shard_map/all_to_all | solution.py:100
  54.5 10.1 %all-to-all-start.5 = ((s32[4,128,1]{1,2,0:T(1,128)}), s32[4,128,1]{1,2,0:T(1,128)S(1)}, u32[]{:S(2)}, u32[]{:S(2)}) async-start(s32[4,128,1]{1,2,0:T(1,128)} %bitcast.26), calls=%async_computation.5 | async-start | bytes 4096 | tf_op jit(solution)/shard_map/all_to_all | solution.py:90
  64.5 14.0 %all-to-all-start.7 = ((s32[1,16,16]{2,0,1:T(1,128)}), s32[1,16,16]{2,0,1:T(1,128)S(1)}, u32[]{:S(2)}, u32[]{:S(2)}) async-start(s32[1,16,16]{2,0,1:T(1,128)} %all_to_all.80), calls=%async_computation.7 | async-start | bytes 16384 | tf_op jit(solution)/shard_map/all_to_all | solution.py:101
  78.5 10.1 %all-to-all-start.4 = ((f32[4,128,128]{2,1,0:T(8,128)}), f32[4,128,128]{2,1,0:T(8,128)S(1)}, u32[]{:S(2)}, u32[]{:S(2)}) async-start(f32[4,128,128]{2,1,0:T(8,128)} %bitcast.30), calls=%async_computation.4 | async-start | bytes 524288 | tf_op jit(solution)/shard_map/all_to_all | solution.py:88
  88.5 25.7 %all-to-all-start.2 = ((f32[1024,16,16]{0,2,1:T(8,128)}), f32[1024,16,16]{0,2,1:T(8,128)S(1)}, u32[]{:S(2)}, u32[]{:S(2)}) async-start(f32[1024,16,16]{0,2,1:T(8,128)} %bitcast.19), calls=%async_computation.2 | async-start | bytes 2097152 | tf_op jit(solution)/shard_map/all_to_all | solution.py:98
  114.3 6.4 %copy-start.2 = (f32[1,1024,256]{2,1,0:T(8,128)S(1)}, f32[1,1024,256]{2,1,0:T(8,128)}, u32[]{:S(2)}) copy-start(f32[1,1024,256]{2,1,0:T(8,128)} %param.15) | copy-start | bytes 3145732
  114.3 29.3 %all-to-all-start.6 = ((f32[1024,16,16]{0,2,1:T(8,128)}), f32[1024,16,16]{0,2,1:T(8,128)S(1)}, u32[]{:S(2)}, u32[]{:S(2)}) async-start(f32[1024,16,16]{0,2,1:T(8,128)} %bitcast.33), calls=%async_computation.6 | async-start | bytes 2097152 | tf_op jit(solution)/shard_map/all_to_all | solution.py:99
  120.6 72.7 %all-reduce.5.cloned.1.call-start = ((), (), s32[]{:S(2)}) async-start(), calls=%async_computation.8 | async-start | bytes 524288 | tf_op jit(solution)/shard_map/psum | solution.py:18
  148.1 278.3 %all-reduce.7.cloned.1.call-start = ((), (), s32[]{:S(2)}) async-start(), calls=%async_computation.9 | async-start | bytes 2097152 | tf_op jit(solution)/shard_map/psum | solution.py:18
  193.3 1.2 copy-start.1
  266.1 214.8 %all-reduce.9.cloned.1.call-start = ((), (), s32[]{:S(2)}) async-start(), calls=%async_computation.10 | async-start | bytes 524288 | tf_op jit(solution)/shard_map/psum | solution.py:140
  429.0 51.9 %copy-start = (f32[1024,256]{0,1:T(8,128)S(1)}, f32[1024,256]{0,1:T(8,128)}, u32[]{:S(2)}) copy-start(f32[1024,256]{0,1:T(8,128)} %all-reduce.7.cloned.1.call-done) | copy-start | bytes 3145732
Sparse Core Ops, SparseCore 0:
  148.2 45.0 all-reduce.4
  266.2 160.1 all-reduce.6
  430.0 50.8 all-reduce.8
where the time goes:
time: 500 us; the launch traced here: 491 us
  waiting for transfers between devices  297 us (59%)
  other arithmetic  69.5 us (14%)
  local copies, waits for them, and re-layouts  57.1 us (11%)
  starting transfers between devices  46.5 us (9%)
  between operations  15.5 us (3%)
  matrix products  5.37 us (1%)
    psum x2, waiting for transfers between devices, spread(): return lax.psum(block, axis)  205 us
    psum x1, waiting for transfers between devices, per_device(): right_factor = lax.psum(masked_part, 'row')  51 us
    another operation x7, other arithmetic, per_device(): factor = jnp.linalg.cholesky(pivot)  34.7 us
    another operation x3, other arithmetic, per_device(): jax.scipy.linalg.solve_triangular(factor, column_part.T, lower=True)  20.4 us
    all_to_all x1, waiting for transfers between devices, extend_add(): lax.all_to_all(packed_cols[1], 'col', split_axis=1, concat_axis=1, tiled=...  15.7 us
    all_to_all x1, waiting for transfers between devices, extend_add(): lax.all_to_all(packed_cols[0], 'col', split_axis=1, concat_axis=1, tiled=...  11.4 us
  transfers between devices with their start and end apart: 13, of which 8 were waited for; matrix products, arithmetic and copies ran while one was open for 9% of the time, Pallas kernels for 0%

commit v1 on v0

v1 whole, which is shorter than its diff:
```python
import functools

import jax
import jax.numpy as jnp
from jax import lax
from jax.experimental import pallas as pl
from jax.experimental.pallas import tpu as pltpu
from jax.sharding import PartitionSpec as P

PW = 256
ROWS = 4
COLS = 16
RB = 1024
CB = 256
UR = 512
UCB = 128
CAPR = 128
CAPC = 16
MESH = pl.DeviceIdType.MESH
F32 = jnp.float32
BF16 = jnp.bfloat16
VMEM_LIMIT = 48 * 1024 * 1024


def parts3(x):
    hi = x.astype(BF16)
    rest = x - hi.astype(F32)
    mid = rest.astype(BF16)
    low = (rest - mid.astype(F32)).astype(BF16)
    return hi, mid, low


def dot_nt(a, b):
    return lax.dot_general(a, b, (((1,), (1,)), ((), ())), preferred_element_type=F32)


def dot_nn(a, b):
    return lax.dot_general(a, b, (((1,), (0,)), ((), ())), preferred_element_type=F32)


def dot_tn(a, b):
    return lax.dot_general(a, b, (((0,), (0,)), ((), ())), preferred_element_type=F32)


def split2(x):
    hi = x.astype(BF16)
    return hi, (x - hi.astype(F32)).astype(BF16)


def dot3(dot, a, b):
    ah, al = split2(a)
    bh, bl = split2(b)
    return dot(ah, bh) + (dot(ah, bl) + dot(al, bh))


def iota(shape, dim):
    return lax.broadcasted_iota(jnp.int32, shape, dim)


def onehot(rows, index):
    return (iota((rows, index.shape[1]), 0) == index).astype(F32).astype(BF16)


def before(n):
    return (iota((n, n), 0) < iota((n, n), 1)).astype(F32).astype(BF16)


def ranked_slot(dest, groups, cap):
    hit = iota((groups, dest.shape[1]), 0) == dest
    hits = hit.astype(F32)
    count = dot_nn(hits.astype(BF16), before(dest.shape[1]))
    rank = jnp.sum(jnp.where(hit, count, 0.0), axis=0, keepdims=True)
    return dest * cap + rank.astype(jnp.int32)


def pack_kernel(pos, u0, u1, m_ref, x_ref):
    r = pos[0]
    c = pos[1]
    for k in range(2):
        u_ref = u0 if k == 0 else u1
        mr = m_ref[k : k + 1, pl.ds(pl.multiple_of(r * UR, UR), UR)]
        mc = m_ref[k : k + 1, pl.ds(pl.multiple_of(c * UCB, UCB), UCB)]
        rp = onehot(UR, ranked_slot(mr // RB, 8, CAPR))
        cp = onehot(COLS * CAPC, ranked_slot(mc // CB, COLS, CAPC))
        x = None
        for part in parts3(u_ref[...]):
            t = dot_nt(cp, part).astype(BF16)
            piece = dot_nt(t, rp)
            x = piece if x is None else x + piece
        for dst in range(ROWS):
            x_ref[dst * COLS : (dst + 1) * COLS, k] = x[:, dst * CAPR : (dst + 1) * CAPR].reshape(COLS, CAPC, CAPR)


def exchange_kernel(x_ref, y_ref, send_sem, recv_sem, local_sem):
    r = lax.axis_index("row")
    c = lax.axis_index("col")
    me = r * COLS + c
    n = ROWS * COLS
    barrier = pltpu.get_barrier_semaphore()

    def greet(o, _):
        t = lax.rem(me + o, n)
        pl.semaphore_signal(
            barrier, inc=1, device_id={"row": t // COLS, "col": t % COLS}, device_id_type=MESH
        )
        return 0

    lax.fori_loop(1, n, greet, 0)
    pl.semaphore_wait(barrier, n - 1)

    def send(o, _):
        t = lax.rem(me + o, n)
        tr = t // COLS
        tc = t % COLS
        pltpu.make_async_remote_copy(
            src_ref=x_ref.at[t],
            dst_ref=y_ref.at[me],
            send_sem=send_sem,
            recv_sem=recv_sem,
            device_id={"row": tr, "col": tc},
            device_id_type=MESH,
        ).start()
        return 0

    lax.fori_loop(1, n, send, 0)
    own = pltpu.make_async_copy(x_ref.at[me], y_ref.at[me], local_sem)
    own.start()
    own.wait()

    every = pltpu.make_async_remote_copy(
        src_ref=x_ref.at[pl.ds(0, n - 1)],
        dst_ref=y_ref.at[pl.ds(0, n - 1)],
        send_sem=send_sem,
        recv_sem=recv_sem,
        device_id={"row": lax.rem(r + 1, ROWS), "col": c},
        device_id_type=MESH,
    )
    every.wait_recv()
    every.wait_send()


def unpack_kernel(pos, y_ref, m_ref, m16_ref, f_ref, a_ref, top_ref):
    r = pos[0]
    c = pos[1]
    mi = jnp.concatenate(
        [m_ref[k : k + 1, s * UR : (s + 1) * UR] for k in range(2) for s in range(ROWS)], axis=0
    )
    hit = (mi // RB) == r
    rank = dot_nn(hit.astype(F32).astype(BF16), before(UR)).astype(jnp.int32)
    slot = jnp.where(hit, rank, -1)
    mj = m16_ref[...]
    hit16 = (mj // CB) == c
    rank16 = dot_nn(hit16.astype(F32).astype(BF16), before(UCB)).astype(jnp.int32)
    slot16 = jnp.where(hit16, rank16 + CAPC * (iota((2 * COLS, UCB), 0) % COLS), -1)
    total = f_ref[...]
    eight = iota((8, 1), 0)
    for k in range(2):
        pieces = []
        for s in range(ROWS):
            row = k * ROWS + s
            g = onehot(CAPR, slot[row : row + 1, :])
            v = mi[row : row + 1, :] % RB
            vals = jnp.where(eight == 0, v // 256, v % 256).astype(F32).astype(BF16)
            got = dot_nt(vals, g)
            pieces.append(got[0:1, :] * 256.0 + got[1:2, :])
        rloc = jnp.concatenate(pieces, axis=1).astype(jnp.int32)
        tslot = jnp.concatenate([slot16[k * COLS + s : k * COLS + s + 1, :] for s in range(COLS)], axis=1)
        g = onehot(COLS * CAPC, tslot)
        v = (m_ref[k : k + 1, :] % CB).astype(F32).astype(BF16)
        got = dot_nt(jnp.broadcast_to(v, (8, COLS * UCB)), g)
        qloc = got[0:1, :].astype(jnp.int32)
        rpl = onehot(RB, rloc)
        cpl = onehot(CB, qloc)
        y = jnp.concatenate(
            [y_ref[s * COLS : (s + 1) * COLS, k].reshape(COLS * CAPC, CAPR) for s in range(ROWS)], axis=1
        )
        for part in parts3(y):
            w = dot_nn(cpl, part).astype(BF16)
            total = total + dot_nt(rpl, w)
    a_ref[...] = total
    top_ref[...] = total[:PW, :]


def spread_kernel(top_ref, xb_ref, pr_ref, pv_ref, s_sem, r_sem, l_sem):
    r = lax.axis_index("row")
    c = lax.axis_index("col")
    y = c // 4
    z = c % 4
    barrier = pltpu.get_barrier_semaphore()
    for o in range(1, 4):
        for target in (
            {"row": (r + o) % 4, "col": c},
            {"row": r, "col": ((y + o) % 4) * 4 + z},
            {"row": r, "col": y * 4 + (z + o) % 4},
        ):
            pl.semaphore_signal(barrier, inc=1, device_id=target, device_id_type=MESH)
    pl.semaphore_wait(barrier, 9)

    def remote(src, dst, i, j, target):
        return pltpu.make_async_remote_copy(
            src_ref=src, dst_ref=dst, send_sem=s_sem.at[i], recv_sem=r_sem.at[j],
            device_id=target, device_id_type=MESH,
        )

    @pl.when(r == 0)
    def _():
        for o in range(1, 4):
            remote(top_ref, xb_ref, o - 1, 0, {"row": (r + o) % 4, "col": c}).start()
        cp = pltpu.make_async_copy(top_ref, xb_ref, l_sem)
        cp.start()
        cp.wait()

    @pl.when(r != 0)
    def _():
        remote(top_ref, xb_ref, 0, 0, {"row": 0, "col": c}).wait_recv()

    @pl.when(c == 0)
    def _():
        for o in range(1, 4):
            remote(xb_ref, pv_ref, 2 + o, 1, {"row": r, "col": o * 4}).start()
        cp = pltpu.make_async_copy(xb_ref, pv_ref, l_sem)
        cp.start()
        cp.wait()

    @pl.when(y == r)
    def _():
        for o in range(1, 4):
            remote(xb_ref, pr_ref.at[z], 5 + o, 2, {"row": r, "col": ((y + o) % 4) * 4 + z}).start()
        cp = pltpu.make_async_copy(xb_ref, pr_ref.at[z], l_sem)
        cp.start()
        cp.wait()

    @pl.when(z == 0)
    def _():
        @pl.when(y != 0)
        def _():
            remote(xb_ref, pv_ref, 0, 1, {"row": r, "col": 0}).wait_recv()

        for o in range(1, 4):
            remote(pv_ref, pv_ref, 8 + o, 1, {"row": r, "col": y * 4 + o}).start()

    @pl.when(y != r)
    def _():
        remote(xb_ref, pr_ref.at[z], 0, 2, {"row": r, "col": r * 4 + z}).wait_recv()

    for o in range(1, 4):
        remote(
            pr_ref.at[z], pr_ref.at[z], 11 + o, 2 + o, {"row": r, "col": y * 4 + (z + o) % 4}
        ).start()

    @pl.when(z != 0)
    def _():
        remote(pv_ref, pv_ref, 0, 1, {"row": r, "col": y * 4}).wait_recv()

    for o in range(1, 4):
        remote(pr_ref.at[z], pr_ref.at[(z - o) % 4], 0, 2 + o, {"row": r, "col": c}).wait_recv()

    @pl.when(r == 0)
    def _():
        for o in range(1, 4):
            remote(top_ref, xb_ref, o - 1, 0, {"row": 1, "col": c}).wait_send()

    @pl.when(c == 0)
    def _():
        for o in range(1, 4):
            remote(xb_ref, pv_ref, 2 + o, 1, {"row": r, "col": 4}).wait_send()

    @pl.when(y == r)
    def _():
        for o in range(1, 4):
            remote(xb_ref, pr_ref.at[z], 5 + o, 2, {"row": r, "col": 4}).wait_send()

    @pl.when(z == 0)
    def _():
        for o in range(1, 4):
            remote(pv_ref, pv_ref, 8 + o, 1, {"row": r, "col": 1}).wait_send()

    for o in range(1, 4):
        remote(pr_ref.at[z], pr_ref.at[z], 11 + o, 2 + o, {"row": r, "col": 1}).wait_send()


NB = 8


def factorize(pv_ref, m_ref):
    n = PW
    m_ref[:, :n] = pv_ref[...]
    m_ref[:, n:] = (iota((n, n), 0) == iota((n, n), 1)).astype(F32)
    sub = iota((NB, 1), 0)
    for b in range(0, n, NB):
        d = m_ref[b : b + NB, (b // 128) * 128 : (b // 128) * 128 + 128]
        rows = m_ref[b : b + NB, :]
        at = b % 128
        for k in range(NB):
            col = d[:, at + k : at + k + 1]
            piv = lax.rsqrt(d[k : k + 1, at + k : at + k + 1])
            mul = jnp.where(sub > k, col * piv, 0.0)
            rk = rows[k : k + 1, :] * piv
            dk = d[k : k + 1, :] * piv
            rows = jnp.where(sub == k, rk, rows - mul * rk)
            d = jnp.where(sub == k, dk, d - mul * dk)
        rows = jnp.where(iota((NB, 2 * n), 1) < b + iota((NB, 2 * n), 0), 0.0, rows)
        m_ref[b : b + NB, :] = rows
        if b + NB < n:
            left = rows[:, :n]
            upd = lax.dot_general(
                left, rows, (((0,), (0,)), ((), ())), preferred_element_type=F32,
                precision=lax.Precision.HIGHEST,
            )
            m_ref[b + NB :, :] = m_ref[b + NB :, :] - upd[b + NB :, :]


def final_kernel(pos, a_ref, xb_ref, pr_ref, pv_ref, o_ref, m_ref):
    r = pos[0]
    c = pos[1]
    factorize(pv_ref, m_ref)
    inv = m_ref[:, PW:]

    @pl.when(c == 0)
    def _():
        for s in range(4):
            o_ref[s * 256 : (s + 1) * 256, :] = lax.dot_general(
                pr_ref[s], inv, (((0,), (1,)), ((), ())), preferred_element_type=F32,
                precision=lax.Precision.HIGHEST,
            )

        @pl.when(r == 0)
        def _():
            o_ref[:PW, :] = m_ref[:, :PW].T

    @pl.when(c != 0)
    def _():
        right = dot3(dot_nn, inv, xb_ref[...])
        for s in range(4):
            left = dot3(dot_nn, inv, pr_ref[s])
            o_ref[s * 256 : (s + 1) * 256, :] = a_ref[s * 256 : (s + 1) * 256, :] - dot3(
                dot_tn, left, right
            )

        @pl.when(r == 0)
        def _():
            o_ref[:PW, :] = jnp.zeros((PW, CB), F32)


def vm():
    return pl.BlockSpec(memory_space=pltpu.VMEM)


def sm():
    return pl.BlockSpec(memory_space=pltpu.SMEM)


def shape(*s):
    return jax.ShapeDtypeStruct(s, F32)


def local_params():
    return pltpu.CompilerParams(vmem_limit_bytes=VMEM_LIMIT)


def remote_params(i):
    return pltpu.CompilerParams(
        vmem_limit_bytes=VMEM_LIMIT, collective_id=i, has_side_effects=True
    )


def pack(pos, u0, u1, maps):
    return pl.pallas_call(
        pack_kernel,
        out_shape=shape(ROWS * COLS, 2, CAPC, CAPR),
        in_specs=[sm(), vm(), vm(), vm()],
        out_specs=vm(),
        compiler_params=local_params(),
    )(pos, u0, u1, maps)


def exchange(x):
    return pl.pallas_call(
        exchange_kernel,
        out_shape=shape(ROWS * COLS, 2, CAPC, CAPR),
        in_specs=[vm()],
        out_specs=vm(),
        scratch_shapes=[pltpu.SemaphoreType.DMA] * 3,
        compiler_params=remote_params(1),
    )(x)


def unpack(pos, y, maps, f):
    return pl.pallas_call(
        unpack_kernel,
        out_shape=[shape(RB, CB), shape(PW, CB)],
        in_specs=[sm(), vm(), vm(), vm(), vm()],
        out_specs=[vm(), vm()],
        compiler_params=local_params(),
    )(pos, y, maps, maps.reshape(2 * COLS, UCB), f)


def spread(top):
    return pl.pallas_call(
        spread_kernel,
        out_shape=[shape(PW, CB), shape(4, PW, CB), shape(PW, CB)],
        in_specs=[vm()],
        out_specs=[vm()] * 3,
        scratch_shapes=[
            pltpu.SemaphoreType.DMA((15,)),
            pltpu.SemaphoreType.DMA((6,)),
            pltpu.SemaphoreType.DMA,
        ],
        compiler_params=remote_params(2),
    )(top)


def final(pos, a, xb, pr, pv):
    return pl.pallas_call(
        final_kernel,
        out_shape=shape(RB, CB),
        in_specs=[sm(), vm(), vm(), vm(), vm()],
        out_specs=vm(),
        scratch_shapes=[pltpu.VMEM((PW, 2 * PW), F32)],
        compiler_params=local_params(),
    )(pos, a, xb, pr, pv)


def per_device(front_matrix, child_updates, child_map):
    pairs = [(s, s ^ 1) for s in range(4)]
    u1 = lax.ppermute(child_updates[0, 1], "front", pairs)
    m1 = lax.ppermute(child_map[0, 1], "front", pairs)
    maps = jnp.stack([child_map[0, 0], m1])
    pos = jnp.stack([lax.axis_index("row"), lax.axis_index("col")]).astype(jnp.int32)
    x = pack(pos, child_updates[0, 0], u1, maps)
    y = exchange(x)
    a, top = unpack(pos, y, maps, front_matrix[0])
    xb, pr, pv = spread(top)
    return final(pos, a, xb, pr, pv)[None]


def solution(mesh):
    in_specs = (P("front", "row", "col"), P("front", None, "row", "col"), P("front", None, None))
    return jax.shard_map(
        per_device, mesh=mesh, in_specs=in_specs, out_specs=P("front", "row", "col"), check_vma=False
    )
```

time: 500 us -> 145 us (0.29)
  the two profiles are of different devices: /device:TPU:8 before, /device:TPU:20 now
where the time goes in v1:
time: 145 us
  Pallas kernels  141 us (97%)
  local copies, waits for them, and re-layouts  1.9 us (1%)
    pallas_call x1, Pallas kernels, spread(): pl.pallas_call(spread_kernel, out_shape=[shape(PW, CB), shape(4, PW, CB),...  59.9 us
    pallas_call x1, Pallas kernels, final(): pl.pallas_call(final_kernel, out_shape=shape(RB, CB), in_specs=[sm(), vm(...  41.1 us
    pallas_call x1, Pallas kernels, exchange(): pl.pallas_call(exchange_kernel, out_shape=shape(ROWS * COLS, 2, CAPC, CAP...  31.6 us
    pallas_call x1, Pallas kernels, unpack(): pl.pallas_call(unpack_kernel, out_shape=[shape(RB, CB), shape(PW, CB)], i...  5.53 us
  transfers between devices with their start and end apart: 2, of which 1 were waited for; matrix products, arithmetic and copies ran while one was open for 1% of the time, Pallas kernels for 0%

profile of v1, /device:TPU:20, one launch (start us, length us, event | category | flops | bytes accessed | tf_op | source)
XLA Modules:
  0.0 144.6 jit_solution(17797340892588196523)
XLA Ops:
  0.0 0.8 slice_bitcast_fusion.2
  0.8 0.1 collective-permute-start.1
  0.9 1.1 slice_bitcast_fusion
  2.0 0.6 collective-permute-start
  2.6 0.1 pad_add_fusion.1.pos
  2.6 0.0 collective-permute-done.1
  2.7 1.0 collective-permute-done.u1
  3.7 2.6 %shard_map.37.x_ref = f32[64,2,16,128]{3,2,1,0:T(8,128)S(1)} custom-call(s32[2]{0:T(128)S(1)} %pad_add_fusion.1.pos, f32[512,128]{1,0:T(8,128)S(1)} %get-tuple-element.16.u0, f32[512,128]{1,0:T(8,128)S(1)} %collective-permute-done.u1, s32[2,2048]{1,0:T(2,128)S(1)} %pad_add_fusion.m_ref), custom_call_target="tpu_custom_call" | custom-call | tf_op jit(solution)/shard_map/pallas_call | solution.py:368
  6.3 0.0 copy-start
  6.3 31.6 %shard_map.38.y_ref = f32[64,2,16,128]{3,2,1,0:T(8,128)S(1)} custom-call(f32[64,2,16,128]{3,2,1,0:T(8,128)S(1)} %shard_map.37.x_ref), custom_call_target="tpu_custom_call" | custom-call | tf_op jit(solution)/shard_map/pallas_call | solution.py:378
  38.0 0.0 copy-done
  38.0 5.5 %shard_map.39 = (f32[1024,256]{1,0:T(8,128)S(1)}, f32[256,256]{1,0:T(8,128)S(1)}) custom-call(s32[2]{0:T(128)S(1)} %pad_add_fusion.1.pos, f32[64,2,16,128]{3,2,1,0:T(8,128)S(1)} %shard_map.38.y_ref, s32[2,2048]{1,0:T(2,128)S(1)} %pad_add_fusion.m_ref, s32[32,128]{1,0:T(8,128)S(1)} %reshape.3.m16_ref, f32[1024,256]{1,0:T(8,128)S(1)} %bitcast.12), custom_call_target="tpu_custom_call" | custom-call | tf_op jit(solution)/shard_map/pallas_call | solution.py:389
  43.5 59.9 %shard_map.40 = (f32[256,256]{1,0:T(8,128)S(1)}, f32[4,256,256]{2,1,0:T(8,128)S(1)}, f32[256,256]{1,0:T(8,128)S(1)}) custom-call(f32[256,256]{1,0:T(8,128)S(1)} %get-tuple-element.11.top_ref), custom_call_target="tpu_custom_call" | custom-call | tf_op jit(solution)/shard_map/pallas_call | solution.py:399
  103.4 41.1 %shard_map.41 = f32[1024,256]{1,0:T(8,128)} custom-call(s32[2]{0:T(128)S(1)} %pad_add_fusion.1.pos, f32[1024,256]{1,0:T(8,128)S(1)} %get-tuple-element.10.a_ref, f32[256,256]{1,0:T(8,128)S(1)} %get-tuple-element.12.xb_ref, f32[4,256,256]{2,1,0:T(8,128)S(1)} %get-tuple-element.13.pr_ref, f32[256,256]{1,0:T(8,128)S(1)} %get-tuple-element.14.pv_ref), custom_call_target="tpu_custom_call" | custom-call | tf_op jit(solution)/shard_map/pallas_call | solution.py:414
  (2 shorter events, 0.0 us)
Async XLA Ops:
  0.8 1.8 %collective-permute-start.1 = (s32[2048]{0:T(1024)S(1)}, s32[2048]{0:T(1024)S(1)}, u32[]{:S(2)}, u32[]{:S(2)}) collective-permute-start(s32[2048]{0:T(1024)S(1)} %bitcast.14), channel_id=1, source_target_pairs={{0,64},{64,0},{128,192},{192,128},{1,65},{65,1},{129,193},{193,129... | collective-permute-start | bytes 24584 | tf_op jit(solution)/shard_map/ppermute | solution.py:427
  2.0 1.7 %collective-permute-start = (f32[512,128]{1,0:T(8,128)S(1)}, f32[512,128]{1,0:T(8,128)S(1)}, u32[]{:S(2)}, u32[]{:S(2)}) collective-permute-start(f32[512,128]{1,0:T(8,128)S(1)} %get-tuple-element.15), channel_id=1, source_target_pairs={{0,64},{64,0},{128,192},{192,128},{1,65},{65,1},{129,193},{193,129... | collective-permute-start | bytes 786440 | tf_op jit(solution)/shard_map/ppermute | solution.py:426
  6.3 31.6 %copy-start = (f32[1,1024,256]{2,1,0:T(8,128)S(1)}, f32[1,1024,256]{2,1,0:T(8,128)}, u32[]{:S(2)}) copy-start(f32[1,1024,256]{2,1,0:T(8,128)} %param.3) | copy-start | bytes 3145732

commit v2 on v1

v2 whole, which is shorter than its diff:
```python
import functools

import jax
import jax.numpy as jnp
from jax import lax
from jax.experimental import pallas as pl
from jax.experimental.pallas import tpu as pltpu
from jax.sharding import PartitionSpec as P

PW = 256
ROWS = 4
COLS = 16
RB = 1024
CB = 256
UR = 512
UCB = 128
CAPR = 128
CAPC = 16
CAPP = 64
OB = 64
MESH = pl.DeviceIdType.MESH
F32 = jnp.float32
BF16 = jnp.bfloat16
VMEM_LIMIT = 48 * 1024 * 1024


def parts3(x):
    hi = x.astype(BF16)
    rest = x - hi.astype(F32)
    mid = rest.astype(BF16)
    low = (rest - mid.astype(F32)).astype(BF16)
    return hi, mid, low


def dot_nt(a, b):
    return lax.dot_general(a, b, (((1,), (1,)), ((), ())), preferred_element_type=F32)


def dot_nn(a, b):
    return lax.dot_general(a, b, (((1,), (0,)), ((), ())), preferred_element_type=F32)


def dot_tn(a, b):
    return lax.dot_general(a, b, (((0,), (0,)), ((), ())), preferred_element_type=F32)


def split2(x):
    hi = x.astype(BF16)
    return hi, (x - hi.astype(F32)).astype(BF16)


def dot3(dot, a, b):
    ah, al = split2(a)
    bh, bl = split2(b)
    return dot(ah, bh) + (dot(ah, bl) + dot(al, bh))


def iota(shape, dim):
    return lax.broadcasted_iota(jnp.int32, shape, dim)


def onehot(rows, index):
    return (iota((rows, index.shape[1]), 0) == index).astype(F32).astype(BF16)


def before(n):
    return (iota((n, n), 0) < iota((n, n), 1)).astype(F32).astype(BF16)


def ranked_slot(dest, groups, cap):
    hit = iota((groups, dest.shape[1]), 0) == dest
    hits = hit.astype(F32)
    count = dot_nn(hits.astype(BF16), before(dest.shape[1]))
    rank = jnp.sum(jnp.where(hit, count, 0.0), axis=0, keepdims=True)
    return dest * cap + rank.astype(jnp.int32)


def pack_kernel(pos, u0, u1, m_ref, m16_ref, x_ref, xp_ref, idx_ref):
    r = pos[0]
    c = pos[1]
    panel = None
    for k in range(2):
        u_ref = u0 if k == 0 else u1
        mr = m_ref[k : k + 1, pl.ds(pl.multiple_of(r * UR, UR), UR)]
        mc = m_ref[k : k + 1, pl.ds(pl.multiple_of(c * UCB, UCB), UCB)]
        rp = onehot(UR, ranked_slot(mr // RB, 8, CAPR))
        cp = onehot(COLS * CAPC, ranked_slot(mc // CB, COLS, CAPC))
        first = mr < PW
        place = ranked_slot(jnp.where(first, 0, 1), 8, 0) + CAPP * k
        pp = onehot(2 * CAPP, jnp.where(first, place, -1))
        x = None
        for part in parts3(u_ref[...]):
            t = dot_nt(cp, part).astype(BF16)
            piece = dot_nt(t, rp)
            x = piece if x is None else x + piece
            piece = dot_nt(t, pp)
            panel = piece if panel is None else panel + piece
        for dst in range(ROWS):
            x_ref[dst * COLS : (dst + 1) * COLS, k] = x[
                :, dst * CAPR : (dst + 1) * CAPR
            ].reshape(COLS, CAPC, CAPR)
    xp_ref[...] = panel.reshape(COLS, CAPC, 2 * CAPP)

    mi = jnp.concatenate(
        [m_ref[k : k + 1, s * UR : (s + 1) * UR] for k in range(2) for s in range(ROWS)], axis=0
    )
    child = iota((8, UR), 0) // ROWS

    def slots(hit, base):
        rank = dot_nn(hit.astype(F32).astype(BF16), before(hit.shape[1])).astype(jnp.int32)
        return jnp.where(hit, rank + base, -1)

    slot = slots((mi // RB) == r, 0)
    pslot = slots(mi < PW, CAPP * child)
    mj = m16_ref[...]
    slot16 = slots((mj // CB) == c, CAPC * (iota((2 * COLS, UCB), 0) % COLS))
    eight = iota((8, 1), 0)
    for k in range(2):
        rows = []
        prows = []
        for s in range(ROWS):
            row = k * ROWS + s
            v = mi[row : row + 1, :]
            vals = jnp.where(eight == 0, (v % RB) // 256, v % 256).astype(F32).astype(BF16)
            got = dot_nt(vals, onehot(CAPR, slot[row : row + 1, :]))
            rows.append(got[0:1, :] * 256.0 + got[1:2, :])
            vals = jnp.broadcast_to((v % 256 + 1).astype(F32).astype(BF16), (8, UR))
            got = dot_nt(vals, onehot(2 * CAPP, pslot[row : row + 1, :]))
            prows.append(got[0:1, :] - 1.0)
        idx_ref[k : k + 1, :] = jnp.concatenate(rows, axis=1).astype(jnp.int32)
        idx_ref[2 + k : 3 + k, :] = jnp.concatenate(prows, axis=1).astype(jnp.int32)
        tslot = jnp.concatenate(
            [slot16[k * COLS + s : k * COLS + s + 1, :] for s in range(COLS)], axis=1
        )
        v = (m_ref[k : k + 1, :] % CB).astype(F32).astype(BF16)
        got = dot_nt(jnp.broadcast_to(v, (8, COLS * UCB)), onehot(COLS * CAPC, tslot))
        idx_ref[4 + k : 5 + k, :CB] = got[0:1, :].astype(jnp.int32)
        idx_ref[4 + k : 5 + k, CB:] = got[0:1, :].astype(jnp.int32)
    idx_ref[6:8, :] = jnp.zeros((2, UR), jnp.int32)


def move_kernel(
    x_ref, xp_ref, idx_ref, f_ref, y_ref, xb_ref, pr_ref, pv_ref, yp_ref,
    ft_ref, xs, xr, ps, prs, bs, br, qs, qr, ds, vs, vr, vt, fs,
):
    r = lax.axis_index("row")
    c = lax.axis_index("col")
    y = c // 4
    z = c % 4
    me = r * COLS + c
    n = ROWS * COLS
    barrier = pltpu.get_barrier_semaphore()

    def at(t):
        return {"row": t // COLS, "col": t % COLS}

    def greet(o, _):
        pl.semaphore_signal(barrier, inc=1, device_id=at(lax.rem(me + o, n)), device_id_type=MESH)
        return 0

    lax.fori_loop(1, n, greet, 0)
    pl.semaphore_wait(barrier, n - 1)

    def remote(src, dst, s_sem, r_sem, row, col):
        return pltpu.make_async_remote_copy(
            src_ref=src, dst_ref=dst, send_sem=s_sem, recv_sem=r_sem,
            device_id={"row": row, "col": col}, device_id_type=MESH,
        )

    def quarter(i):
        return pl.ds(pl.multiple_of(i * 64, 64), 64)

    def sixteenth(i):
        return pl.ds(pl.multiple_of(i * 16, 16), 16)

    top = pltpu.make_async_copy(f_ref.at[0:PW], ft_ref, fs)
    top.start()

    def send_panel(o, _):
        t = lax.rem(c + o, COLS)
        remote(xp_ref.at[t], yp_ref.at[me], ps, prs, 0, t).start()
        return 0

    lax.fori_loop(1, COLS, send_panel, 0)

    @pl.when(r != 0)
    def _():
        remote(xp_ref.at[c], yp_ref.at[me], ps, prs, 0, c).start()

    def bulk(lo, hi):
        def send(o, _):
            t = lax.rem(me + o, n)
            remote(x_ref.at[t], y_ref.at[me], xs, xr, t // COLS, t % COLS).start()
            return 0

        lax.fori_loop(lo, hi, send, 0)

    top.wait()

    @pl.when(r == 0)
    def _():
        yp_ref[pl.ds(me, 1)] = xp_ref[pl.ds(c, 1)]
        remote(yp_ref.at[pl.ds(0, n - 1)], yp_ref.at[pl.ds(0, n - 1)], ps, prs, 1, c).wait_recv()
        total = ft_ref[...]
        src = jnp.concatenate(
            [yp_ref[s * COLS : (s + 1) * COLS].reshape(COLS * CAPC, 2 * CAPP) for s in range(ROWS)],
            axis=1,
        )
        parts = parts3(src)
        for k in range(2):
            rpl = onehot(PW, idx_ref[2 + k : 3 + k, :])
            cpl = onehot(CB, idx_ref[4 + k : 5 + k, :CB])
            for part in parts:
                total = total + dot_nt(rpl, dot_nn(cpl, part).astype(BF16))
        xb_ref[...] = total

        @pl.when(c == 0)
        def _():
            pv_ref[0:16, :] = xb_ref[0:16, :]

            def piece(t, _):
                remote(
                    xb_ref.at[sixteenth(t)], pv_ref.at[sixteenth(t)], vs.at[0], vr.at[0],
                    t // 4, (t % 4) * 4,
                ).start()
                return 0

            lax.fori_loop(1, 16, piece, 0)

        def part_to(q, _):
            remote(
                xb_ref.at[quarter(q)], pr_ref.at[z, quarter(q)], qs, qr.at[z, q], y, q * 4 + z
            ).start()
            return 0

        @pl.when(y == 0)
        def _():
            pr_ref[pl.ds(z, 1), 0:64] = xb_ref[0:64, :].reshape(1, 64, CB)
            lax.fori_loop(1, 4, part_to, 0)

        @pl.when(y != 0)
        def _():
            lax.fori_loop(0, 4, part_to, 0)

        for o in range(1, 4):
            remote(xb_ref, xb_ref, bs.at[o - 1], br, o, c).start()

    mine = 4 * r + y

    @pl.when(z == 0)
    def _():
        @pl.when(mine != 0)
        def _():
            remote(pv_ref.at[sixteenth(mine)], pv_ref.at[sixteenth(mine)], vs.at[0], vr.at[0], r, c).wait_recv()

        for o in range(1, 4):
            remote(
                pv_ref.at[sixteenth(mine)], pv_ref.at[sixteenth(mine)], vt.at[o - 1], vr.at[0], r, y * 4 + o
            ).start()

    @pl.when(z != 0)
    def _():
        remote(pv_ref.at[sixteenth(mine)], pv_ref.at[sixteenth(mine)], vs.at[0], vr.at[0], r, c).wait_recv()

    def plane(o, _):
        t = lax.rem(mine + o, 16)
        remote(
            pv_ref.at[sixteenth(mine)], pv_ref.at[sixteenth(mine)], vs.at[1], vr.at[1],
            t // 4, (t % 4) * 4 + z,
        ).start()
        return 0

    lax.fori_loop(1, 16, plane, 0)

    @pl.when(jnp.logical_or(r != 0, me >= 4))
    def _():
        remote(pr_ref.at[z, quarter(y)], pr_ref.at[z, quarter(y)], qs, qr.at[z, y], r, c).wait_recv()

    def to_y(zz):
        for o in range(1, 4):
            remote(
                pr_ref.at[zz, quarter(y)], pr_ref.at[zz, quarter(y)], ds.at[2], qr.at[zz, y],
                r, lax.rem(y + o, 4) * 4 + z,
            ).start()

    for o in range(1, 4):
        remote(
            pr_ref.at[z, quarter(y)], pr_ref.at[z, quarter(y)], ds.at[1], qr.at[z, y],
            r, y * 4 + lax.rem(z + o, 4),
        ).start()
    to_y(z)
    bulk(1, n)
    for o in range(1, 4):
        zz = lax.rem(z + o, 4)
        remote(pr_ref.at[zz, quarter(y)], pr_ref.at[zz, quarter(y)], qs, qr.at[zz, y], r, c).wait_recv()
        to_y(zz)

    y_ref[pl.ds(me, 1)] = x_ref[pl.ds(me, 1)]

    remote(pv_ref.at[0:240], pv_ref.at[0:240], vs.at[1], vr.at[1], r, c).wait_recv()

    @pl.when(r != 0)
    def _():
        remote(xb_ref, xb_ref, bs.at[0], br, r, c).wait_recv()

    for zz in range(4):
        for o in range(1, 4):
            yy = lax.rem(y + o, 4)
            remote(pr_ref.at[zz, quarter(yy)], pr_ref.at[zz, quarter(yy)], qs, qr.at[zz, yy], r, c).wait_recv()
    remote(x_ref.at[pl.ds(0, n - 1)], y_ref.at[pl.ds(0, n - 1)], xs, xr, r, c).wait_recv()

    remote(x_ref.at[pl.ds(0, n - 1)], y_ref.at[pl.ds(0, n - 1)], xs, xr, r, c).wait_send()
    remote(pv_ref.at[0:240], pv_ref.at[0:240], vs.at[1], vr.at[1], r, c).wait_send()
    remote(pr_ref.at[0, 0:192], pr_ref.at[0, 0:192], ds.at[1], br, r, c).wait_send()
    remote(pr_ref.at[0:3], pr_ref.at[0:3], ds.at[2], br, r, c).wait_send()

    @pl.when(z == 0)
    def _():
        for o in range(1, 4):
            remote(pv_ref.at[0:16], pv_ref.at[0:16], vt.at[o - 1], br, r, c).wait_send()

    @pl.when(r != 0)
    def _():
        remote(xp_ref, yp_ref.at[pl.ds(0, COLS)], ps, prs, r, c).wait_send()

    @pl.when(r == 0)
    def _():
        remote(xp_ref.at[0:15], yp_ref.at[0:15], ps, prs, r, c).wait_send()

        @pl.when(y == 0)
        def _():
            remote(xb_ref.at[0:192], xb_ref.at[0:192], qs, br, r, c).wait_send()

        @pl.when(y != 0)
        def _():
            remote(xb_ref, xb_ref, qs, br, r, c).wait_send()

        @pl.when(c == 0)
        def _():
            remote(xb_ref.at[0:240], xb_ref.at[0:240], vs.at[0], br, r, c).wait_send()

        for o in range(1, 4):
            remote(xb_ref, xb_ref, bs.at[o - 1], br, r, c).wait_send()


def factorize(m_ref, pv):
    n = PW
    m_ref[:, :n] = pv
    m_ref[:, n:] = (iota((n, n), 0) == iota((n, n), 1)).astype(F32)
    for b0 in range(0, n, OB):
        lo = (b0 // 128) * 128
        hi = n + ((b0 + OB - 1) // 128) * 128 + 128
        R = [m_ref[b0 + 8 * i : b0 + 8 * i + 8, lo:hi] for i in range(OB // 8)]
        w = hi - lo
        sub = iota((8, 128), 0)
        sub1 = iota((8, 1), 0)
        for ib in range(OB // 8):
            b = b0 + 8 * ib
            at = b - lo
            C = [[jnp.broadcast_to(R[i][:, at + k : at + k + 1], (8, 128)) for i in range(ib, OB // 8)] for k in range(8)]
            for k in range(8):
                piv = jnp.broadcast_to(C[k][0][k : k + 1, :], (8, 128))
                rs = lax.rsqrt(piv)
                mul = [c * rs for c in C[k]]
                mul[0] = jnp.where(sub > k, mul[0], 0.0)
                for j in range(k + 1, 8):
                    t = jnp.broadcast_to(C[j][0][k : k + 1, :], (8, 128)) * rs
                    C[j] = [c - m * t for c, m in zip(C[j], mul)]
                rk = jnp.concatenate([jnp.broadcast_to(R[ib][k:k+1, q*128:(q+1)*128], (8,128)) * rs for q in range(w // 128)], axis=1)
                for i in range(ib, OB // 8):
                    m = jnp.concatenate([mul[i - ib]] * (w // 128), axis=1)
                    new = R[i] - m * rk
                    if i == ib:
                        new = jnp.where(jnp.concatenate([sub] * (w // 128), axis=1) == k, rk, new)
                    R[i] = new
        rows = jnp.concatenate(R, axis=0)
        below = (iota((OB, w), 1) + lo) < (b0 + iota((OB, w), 0))
        rows = jnp.where(below, 0.0, rows)
        m_ref[b0 : b0 + OB, lo:hi] = rows
        if lo:
            m_ref[b0 : b0 + OB, :lo] = jnp.zeros((OB, lo), F32)
        nb = b0 + OB
        if nb < n:
            l2 = (nb // 128) * 128
            upd = lax.dot_general(rows[:, l2 - lo : n - lo], rows[:, l2 - lo :], (((0,), (0,)), ((), ())), preferred_element_type=F32, precision=lax.Precision.HIGHEST)
            m_ref[nb:, l2:hi] = m_ref[nb:, l2:hi] - upd[nb - l2 :, :]


def final_kernel(pos, y_ref, idx_ref, f_ref, xb_ref, pr_ref, pv_ref, o_ref, m_ref):
    r = pos[0]
    c = pos[1]
    factorize(m_ref, pv_ref[...])
    inv = m_ref[:, PW:]

    @pl.when(c == 0)
    def _():
        for s in range(4):
            o_ref[s * 256 : (s + 1) * 256, :] = lax.dot_general(
                pr_ref[s], inv, (((0,), (1,)), ((), ())), preferred_element_type=F32,
                precision=lax.Precision.HIGHEST,
            )

        @pl.when(r == 0)
        def _():
            o_ref[:PW, :] = m_ref[:, :PW].T

    @pl.when(c != 0)
    def _():
        right = dot3(dot_nn, inv, xb_ref[...])
        ws = []
        for k in range(2):
            cpl = onehot(CB, idx_ref[4 + k : 5 + k, :CB])
            src = jnp.concatenate(
                [y_ref[s * COLS : (s + 1) * COLS, k].reshape(COLS * CAPC, CAPR) for s in range(ROWS)],
                axis=1,
            )
            ws.append([dot_nn(cpl, part).astype(BF16) for part in parts3(src)])
        for s in range(4):
            rows = slice(s * 256, (s + 1) * 256)
            left = dot3(dot_nn, inv, pr_ref[s])
            total = f_ref[rows, :] - dot3(dot_tn, left, right)
            for k in range(2):
                rpl = onehot(PW, idx_ref[k : k + 1, :] - s * 256)
                for w in ws[k]:
                    total = total + dot_nt(rpl, w)
            o_ref[rows, :] = total

        @pl.when(r == 0)
        def _():
            o_ref[:PW, :] = jnp.zeros((PW, CB), F32)


def vm():
    return pl.BlockSpec(memory_space=pltpu.VMEM)


def sm():
    return pl.BlockSpec(memory_space=pltpu.SMEM)


def shape(*s):
    return jax.ShapeDtypeStruct(s, F32)


def local_params():
    return pltpu.CompilerParams(vmem_limit_bytes=VMEM_LIMIT)


def remote_params(i):
    return pltpu.CompilerParams(
        vmem_limit_bytes=VMEM_LIMIT, collective_id=i, has_side_effects=True
    )


def pack(pos, u0, u1, maps):
    return pl.pallas_call(
        pack_kernel,
        out_shape=[
            shape(ROWS * COLS, 2, CAPC, CAPR),
            shape(COLS, CAPC, 2 * CAPP),
            jax.ShapeDtypeStruct((8, UR), jnp.int32),
        ],
        in_specs=[sm(), vm(), vm(), vm(), vm()],
        out_specs=[vm()] * 3,
        compiler_params=local_params(),
    )(pos, u0, u1, maps, maps.reshape(2 * COLS, UCB))


def move(x, xp, idx, f):
    dma = pltpu.SemaphoreType.DMA
    return pl.pallas_call(
        move_kernel,
        out_shape=[
            shape(ROWS * COLS, 2, CAPC, CAPR),
            shape(PW, CB),
            shape(4, PW, CB),
            shape(PW, CB),
        ],
        in_specs=[vm(), vm(), vm(), pl.BlockSpec(memory_space=pl.ANY)],
        out_specs=[vm()] * 4,
        scratch_shapes=[
            pltpu.VMEM((ROWS * COLS, CAPC, 2 * CAPP), F32),
            pltpu.VMEM((PW, CB), F32),
            dma, dma, dma, dma, dma((3,)), dma, dma, dma((4, 4)), dma((3,)), dma((2,)), dma((2,)),
            dma((3,)), dma,
        ],
        compiler_params=remote_params(1),
    )(x, xp, idx, f)


def final(pos, y, idx, f, xb, pr, pv):
    return pl.pallas_call(
        final_kernel,
        out_shape=shape(RB, CB),
        in_specs=[sm()] + [vm()] * 6,
        out_specs=vm(),
        scratch_shapes=[pltpu.VMEM((PW, 2 * PW), F32)],
        compiler_params=local_params(),
    )(pos, y, idx, f, xb, pr, pv)


def per_device(front_matrix, child_updates, child_map):
    pairs = [(s, s ^ 1) for s in range(4)]
    u1 = lax.ppermute(child_updates[0, 1], "front", pairs)
    m1 = lax.ppermute(child_map[0, 1], "front", pairs)
    maps = jnp.stack([child_map[0, 0], m1])
    pos = jnp.stack([lax.axis_index("row"), lax.axis_index("col")]).astype(jnp.int32)
    f = front_matrix[0]
    x, xp, idx = pack(pos, child_updates[0, 0], u1, maps)
    y, xb, pr, pv = move(x, xp, idx, f)
    return final(pos, y, idx, f, xb, pr, pv)[None]


def solution(mesh):
    in_specs = (P("front", "row", "col"), P("front", None, "row", "col"), P("front", None, None))
    return jax.shard_map(
        per_device, mesh=mesh, in_specs=in_specs, out_specs=P("front", "row", "col"), check_vma=False
    )
```

time: 145 us -> 79 us (0.54)
  the two profiles are of different devices: /device:TPU:20 before, /device:TPU:12 now
where the time goes in v2:
time: 79 us; the launch traced here: 78.8 us
  Pallas kernels  75 us (95%)
  local copies, waits for them, and re-layouts  1.93 us (2%)
  waiting for transfers between devices  1.04 us (1%)
    pallas_call x1, Pallas kernels, move(): pl.pallas_call(move_kernel, out_shape=[shape(ROWS * COLS, 2, CAPC, CAPR),...  56.5 us
    pallas_call x1, Pallas kernels, final(): pl.pallas_call(final_kernel, out_shape=shape(RB, CB), in_specs=[sm()] + [...  14.2 us
    pallas_call x1, Pallas kernels, pack(): pl.pallas_call(pack_kernel, out_shape=[shape(ROWS * COLS, 2, CAPC, CAPR),...  4.37 us
  transfers between devices with their start and end apart: 2, of which 1 were waited for; matrix products, arithmetic and copies ran while one was open for 1% of the time, Pallas kernels for 0%

profile of v2, /device:TPU:12, one launch (start us, length us, event | category | flops | bytes accessed | tf_op | source)
XLA Modules:
  0.0 78.8 jit_solution(4684001550962911669)
XLA Ops:
  0.0 0.0 copy-start
  0.0 0.8 %slice_bitcast_fusion.2 = (s32[1,2048]{1,0:T(1,128)S(1)}, s32[1,1,2048]{2,1,0:T(1,128)S(1)}) fusion(s32[1,2,2048]{2,1,0:T(2,128)} %param.5), kind=kLoop, calls=%fused_computation.3 | loop fusion | bytes 32768 | tf_op jit(solution)/shard_map/stack;squeeze | solution.py:506
  0.8 0.1 collective-permute-start.1
  0.9 1.1 %slice_bitcast_fusion = (f32[512,128]{1,0:T(8,128)S(1)}, f32[512,128]{1,0:T(8,128)S(1)}) fusion(f32[1,2,512,128]{3,2,1,0:T(8,128)} %param.4), kind=kLoop, calls=%fused_computation | loop fusion | bytes 1048576 | tf_op jit(solution)/shard_map/squeeze | solution.py:504
  2.0 0.6 collective-permute-start
  2.6 0.1 pad_add_fusion.1.pos
  2.7 0.0 collective-permute-done.1
  2.7 1.0 %collective-permute-done.u1 = f32[512,128]{1,0:T(8,128)S(1)} collective-permute-done((f32[512,128]{1,0:T(8,128)S(1)}, f32[512,128]{1,0:T(8,128)S(1)}, u32[]{:S(2)}, u32[]{:S(2)}) %collective-permute-start) | collective-permute-done | bytes 262176 | tf_op jit(solution)/shard_map/ppermute | solution.py:504
  3.8 4.4 %shard_map.37 = (f32[64,2,16,128]{3,2,1,0:T(8,128)S(1)}, f32[16,16,128]{2,1,0:T(8,128)S(1)}, s32[8,512]{1,0:T(8,128)S(1)}) custom-call(s32[2]{0:T(128)S(1)} %pad_add_fusion.1.pos, f32[512,128]{1,0:T(8,128)S(1)} %get-tuple-element.20.u0, f32[512,128]{1,0:T(8,128)S(1)} %collective-permute-done.u1, s32[2,2048]{1,0:T(2,128)S(1)} %pad_add_fusion.m_ref, ...), custom_call_target="tpu_custom_call" | custom-call | tf_op jit(solution)/shard_map/pallas_call | solution.py:456
  8.1 0.0 copy-done
  8.1 56.5 %shard_map.38 = (f32[64,2,16,128]{3,2,1,0:T(8,128)S(1)}, f32[256,256]{1,0:T(8,128)S(1)}, f32[4,256,256]{2,1,0:T(8,128)S(1)}, f32[256,256]{1,0:T(8,128)S(1)}) custom-call(f32[64,2,16,128]{3,2,1,0:T(8,128)S(1)} %get-tuple-element.12.x_ref, f32[16,16,128]{2,1,0:T(8,128)S(1)} %get-tuple-element.13.xp_ref, s32[8,512]{1,0:T(8,128)S(1)} %get-tuple-element.14.idx_ref, ...), custom_call_target="tpu_custom_call" | custom-call | tf_op jit(solution)/shard_map/pallas_call | solution.py:471
  64.6 14.2 %shard_map.39 = f32[1024,256]{1,0:T(8,128)} custom-call(s32[2]{0:T(128)S(1)} %pad_add_fusion.1.pos, f32[64,2,16,128]{3,2,1,0:T(8,128)S(1)} %get-tuple-element.15.y_ref, s32[8,512]{1,0:T(8,128)S(1)} %get-tuple-element.14.idx_ref, f32[1024,256]{1,0:T(8,128)S(1)} %bitcast.13, f32[256,256]{1,0:T(8,128)S(1)} %get-tuple-element.16.xb_ref, ...), custom_call_target="tpu_custom_call" | custom-call | tf_op jit(solution)/shard_map/pallas_call | solution.py:492
  (2 shorter events, 0.0 us)
Async XLA Ops:
  0.0 8.1 %copy-start = (f32[1,1024,256]{2,1,0:T(8,128)S(1)}, f32[1,1024,256]{2,1,0:T(8,128)}, u32[]{:S(2)}) copy-start(f32[1,1024,256]{2,1,0:T(8,128)} %param.3) | copy-start | bytes 3145732
  0.8 1.8 %collective-permute-start.1 = (s32[2048]{0:T(1024)S(1)}, s32[2048]{0:T(1024)S(1)}, u32[]{:S(2)}, u32[]{:S(2)}) collective-permute-start(s32[2048]{0:T(1024)S(1)} %bitcast.15), channel_id=1, source_target_pairs={{0,64},{64,0},{128,192},{192,128},{1,65},{65,1},{129,193},{193,129... | collective-permute-start | bytes 24584 | tf_op jit(solution)/shard_map/ppermute | solution.py:505
  2.0 1.7 %collective-permute-start = (f32[512,128]{1,0:T(8,128)S(1)}, f32[512,128]{1,0:T(8,128)S(1)}, u32[]{:S(2)}, u32[]{:S(2)}) collective-permute-start(f32[512,128]{1,0:T(8,128)S(1)} %get-tuple-element.19), channel_id=1, source_target_pairs={{0,64},{64,0},{128,192},{192,128},{1,65},{65,1},{129,193},{193,129... | collective-permute-start | bytes 786440 | tf_op jit(solution)/shard_map/ppermute | solution.py:504

commit v3 on v2

v3 whole, which is shorter than its diff:
```python
import functools

import jax
import jax.numpy as jnp
from jax import lax
from jax.experimental import pallas as pl
from jax.experimental.pallas import tpu as pltpu
from jax.sharding import PartitionSpec as P

PW = 256
ROWS = 4
COLS = 16
RB = 1024
CB = 256
UR = 512
UCB = 128
CAPR = 128
CAPC = 16
CAPP = 64
OB = 64
MESH = pl.DeviceIdType.MESH
F32 = jnp.float32
BF16 = jnp.bfloat16
VMEM_LIMIT = 48 * 1024 * 1024


def parts3(x):
    hi = x.astype(BF16)
    rest = x - hi.astype(F32)
    mid = rest.astype(BF16)
    low = (rest - mid.astype(F32)).astype(BF16)
    return hi, mid, low


def dot_nt(a, b):
    return lax.dot_general(a, b, (((1,), (1,)), ((), ())), preferred_element_type=F32)


def dot_nn(a, b):
    return lax.dot_general(a, b, (((1,), (0,)), ((), ())), preferred_element_type=F32)


def dot_tn(a, b):
    return lax.dot_general(a, b, (((0,), (0,)), ((), ())), preferred_element_type=F32)


def split2(x):
    hi = x.astype(BF16)
    return hi, (x - hi.astype(F32)).astype(BF16)


def dot3(dot, a, b):
    ah, al = split2(a)
    bh, bl = split2(b)
    return dot(ah, bh) + (dot(ah, bl) + dot(al, bh))


def iota(shape, dim):
    return lax.broadcasted_iota(jnp.int32, shape, dim)


def onehot(rows, index):
    return (iota((rows, index.shape[1]), 0) == index).astype(F32).astype(BF16)


def before(n):
    return (iota((n, n), 0) < iota((n, n), 1)).astype(F32).astype(BF16)


def ranked_slot(dest, groups, cap):
    hit = iota((groups, dest.shape[1]), 0) == dest
    hits = hit.astype(F32)
    count = dot_nn(hits.astype(BF16), before(dest.shape[1]))
    rank = jnp.sum(jnp.where(hit, count, 0.0), axis=0, keepdims=True)
    return dest * cap + rank.astype(jnp.int32)


def factorize(m_ref, pv):
    n = PW
    m_ref[:, :n] = pv
    m_ref[:, n:] = (iota((n, n), 0) == iota((n, n), 1)).astype(F32)
    for b0 in range(0, n, OB):
        lo = (b0 // 128) * 128
        hi = n + ((b0 + OB - 1) // 128) * 128 + 128
        R = [m_ref[b0 + 8 * i : b0 + 8 * i + 8, lo:hi] for i in range(OB // 8)]
        w = hi - lo
        sub = iota((8, 128), 0)
        sub1 = iota((8, 1), 0)
        for ib in range(OB // 8):
            b = b0 + 8 * ib
            at = b - lo
            C = [[jnp.broadcast_to(R[i][:, at + k : at + k + 1], (8, 128)) for i in range(ib, OB // 8)] for k in range(8)]
            for k in range(8):
                piv = jnp.broadcast_to(C[k][0][k : k + 1, :], (8, 128))
                rs = lax.rsqrt(piv)
                mul = [c * rs for c in C[k]]
                mul[0] = jnp.where(sub > k, mul[0], 0.0)
                for j in range(k + 1, 8):
                    t = jnp.broadcast_to(C[j][0][k : k + 1, :], (8, 128)) * rs
                    C[j] = [c - m * t for c, m in zip(C[j], mul)]
                rk = jnp.concatenate([jnp.broadcast_to(R[ib][k:k+1, q*128:(q+1)*128], (8,128)) * rs for q in range(w // 128)], axis=1)
                for i in range(ib, OB // 8):
                    m = jnp.concatenate([mul[i - ib]] * (w // 128), axis=1)
                    new = R[i] - m * rk
                    if i == ib:
                        new = jnp.where(jnp.concatenate([sub] * (w // 128), axis=1) == k, rk, new)
                    R[i] = new
        rows = jnp.concatenate(R, axis=0)
        below = (iota((OB, w), 1) + lo) < (b0 + iota((OB, w), 0))
        rows = jnp.where(below, 0.0, rows)
        m_ref[b0 : b0 + OB, lo:hi] = rows
        if lo:
            m_ref[b0 : b0 + OB, :lo] = jnp.zeros((OB, lo), F32)
        nb = b0 + OB
        if nb < n:
            l2 = (nb // 128) * 128
            upd = lax.dot_general(rows[:, l2 - lo : n - lo], rows[:, l2 - lo :], (((0,), (0,)), ((), ())), preferred_element_type=F32, precision=lax.Precision.HIGHEST)
            m_ref[nb:, l2:hi] = m_ref[nb:, l2:hi] - upd[nb - l2 :, :]


def kernel(
    m_ref, u_ref, f_hbm, o_ref,
    u0_ref, u1_ref, mp_ref, f_ref, x_ref, y_ref, xp_ref, yp_ref, xb_ref, pr_ref, pv_ref, e_ref,
    lo_sem, us, ur, xs, xr, ps, prs, bs, br, qs, qr, ds, vs, vr, vt,
):
    f = lax.axis_index("front")
    r = lax.axis_index("row")
    c = lax.axis_index("col")
    y = c // 4
    z = c % 4
    me = r * COLS + c
    n = ROWS * COLS
    other = f + 1 - 2 * (f % 2)
    load_u = pltpu.make_async_copy(u_ref.at[0], u0_ref, lo_sem.at[0])
    load_u.start()
    load_f = pltpu.make_async_copy(f_hbm, f_ref, lo_sem.at[1])
    load_f.start()

    barrier = pltpu.get_barrier_semaphore()
    partner = {"front": other, "row": r, "col": c}
    pl.semaphore_signal(barrier, inc=1, device_id=partner, device_id_type=MESH)

    def greet(o, _):
        t = lax.rem(me + o, n)
        pl.semaphore_signal(
            barrier, inc=1, device_id={"row": t // COLS, "col": t % COLS}, device_id_type=MESH
        )
        return 0

    lax.fori_loop(1, n, greet, 0)
    pl.semaphore_wait(barrier, n)

    def remote(src, dst, s_sem, r_sem, row, col):
        return pltpu.make_async_remote_copy(
            src_ref=src, dst_ref=dst, send_sem=s_sem, recv_sem=r_sem,
            device_id={"row": row, "col": col}, device_id_type=MESH,
        )

    def quarter(i):
        return pl.ds(pl.multiple_of(i * 64, 64), 64)

    def sixteenth(i):
        return pl.ds(pl.multiple_of(i * 16, 16), 16)

    swap_m = pltpu.make_async_remote_copy(
        src_ref=m_ref, dst_ref=mp_ref, send_sem=us.at[0], recv_sem=ur.at[0],
        device_id=partner, device_id_type=MESH,
    )
    swap_m.start()
    swap_u = pltpu.make_async_remote_copy(
        src_ref=u_ref.at[1], dst_ref=u1_ref, send_sem=us.at[1], recv_sem=ur.at[1],
        device_id=partner, device_id_type=MESH,
    )
    swap_u.start()

    def maps(k):
        return m_ref if k == 0 else mp_ref

    panel = None
    columns = []
    for k in range(2):
        if k == 0:
            load_u.wait()
        else:
            swap_m.wait()
            swap_u.wait()
        mr = maps(k)[k : k + 1, pl.ds(pl.multiple_of(r * UR, UR), UR)]
        mc = maps(k)[k : k + 1, pl.ds(pl.multiple_of(c * UCB, UCB), UCB)]
        cp = onehot(COLS * CAPC, ranked_slot(mc // CB, COLS, CAPC))
        first = mr < PW
        place = ranked_slot(jnp.where(first, 0, 1), 8, 0) + CAPP * k
        pp = onehot(2 * CAPP, jnp.where(first, place, -1))
        values = u0_ref[...] if k == 0 else u1_ref[...]
        columns.append([dot_nt(cp, part).astype(BF16) for part in parts3(values)])
        for t in columns[k]:
            piece = dot_nt(t, pp)
            panel = piece if panel is None else panel + piece
    xp_ref[...] = panel.reshape(COLS, CAPC, 2 * CAPP)

    def send_panel(o, _):
        t = lax.rem(c + o, COLS)
        remote(xp_ref.at[t], yp_ref.at[me], ps, prs, 0, t).start()
        return 0

    lax.fori_loop(1, COLS, send_panel, 0)

    @pl.when(r != 0)
    def _():
        remote(xp_ref.at[c], yp_ref.at[me], ps, prs, 0, c).start()

    for k in range(2):
        mr = maps(k)[k : k + 1, pl.ds(pl.multiple_of(r * UR, UR), UR)]
        rp = onehot(UR, ranked_slot(mr // RB, 8, CAPR))
        x = None
        for t in columns[k]:
            piece = dot_nt(t, rp)
            x = piece if x is None else x + piece
        for dst in range(ROWS):
            x_ref[dst * COLS : (dst + 1) * COLS, k] = x[
                :, dst * CAPR : (dst + 1) * CAPR
            ].reshape(COLS, CAPC, CAPR)

    def send_bulk(o, _):
        t = lax.rem(me + o, n)
        remote(x_ref.at[t], y_ref.at[me], xs, xr, t // COLS, t % COLS).start()
        return 0

    lax.fori_loop(1, n, send_bulk, 0)
    y_ref[pl.ds(me, 1)] = x_ref[pl.ds(me, 1)]

    mi = jnp.concatenate(
        [maps(k)[k : k + 1, s * UR : (s + 1) * UR] for k in range(2) for s in range(ROWS)], axis=0
    )
    mj = jnp.concatenate(
        [maps(k)[k : k + 1, s * UCB : (s + 1) * UCB] for k in range(2) for s in range(COLS)], axis=0
    )
    child = iota((8, UR), 0) // ROWS

    def slots(hit, base):
        rank = dot_nn(hit.astype(F32).astype(BF16), before(hit.shape[1])).astype(jnp.int32)
        return jnp.where(hit, rank + base, -1)

    slot = slots((mi // RB) == r, 0)
    pslot = slots(mi < PW, CAPP * child)
    slot16 = slots((mj // CB) == c, CAPC * (iota((2 * COLS, UCB), 0) % COLS))
    eight = iota((8, 1), 0)
    row_of = []
    prow_of = []
    col_of = []
    for k in range(2):
        rows = []
        prows = []
        for s in range(ROWS):
            row = k * ROWS + s
            v = mi[row : row + 1, :]
            vals = jnp.where(eight == 0, (v % RB) // 256, v % 256).astype(F32).astype(BF16)
            got = dot_nt(vals, onehot(CAPR, slot[row : row + 1, :]))
            rows.append(got[0:1, :] * 256.0 + got[1:2, :])
            vals = jnp.broadcast_to((v % 256 + 1).astype(F32).astype(BF16), (8, UR))
            got = dot_nt(vals, onehot(2 * CAPP, pslot[row : row + 1, :]))
            prows.append(got[0:1, :] - 1.0)
        row_of.append(jnp.concatenate(rows, axis=1).astype(jnp.int32))
        prow_of.append(jnp.concatenate(prows, axis=1).astype(jnp.int32))
        tslot = jnp.concatenate(
            [slot16[k * COLS + s : k * COLS + s + 1, :] for s in range(COLS)], axis=1
        )
        v = (maps(k)[k : k + 1, :] % CB).astype(F32).astype(BF16)
        got = dot_nt(jnp.broadcast_to(v, (8, COLS * UCB)), onehot(COLS * CAPC, tslot))
        col_of.append(got[0:1, :].astype(jnp.int32))
    cpl = [onehot(CB, col_of[k]) for k in range(2)]

    load_f.wait()

    @pl.when(r == 0)
    def _():
        yp_ref[pl.ds(me, 1)] = xp_ref[pl.ds(c, 1)]
        remote(yp_ref.at[pl.ds(0, n - 1)], yp_ref.at[pl.ds(0, n - 1)], ps, prs, 1, c).wait_recv()
        total = f_ref[:PW, :]
        src = jnp.concatenate(
            [yp_ref[s * COLS : (s + 1) * COLS].reshape(COLS * CAPC, 2 * CAPP) for s in range(ROWS)],
            axis=1,
        )
        parts = parts3(src)
        for k in range(2):
            rpl = onehot(PW, prow_of[k])
            for part in parts:
                total = total + dot_nt(rpl, dot_nn(cpl[k], part).astype(BF16))
        xb_ref[...] = total

        @pl.when(c == 0)
        def _():
            pv_ref[0:16, :] = xb_ref[0:16, :]

            def piece(t, _):
                remote(
                    xb_ref.at[sixteenth(t)], pv_ref.at[sixteenth(t)], vs.at[0], vr.at[0],
                    t // 4, (t % 4) * 4,
                ).start()
                return 0

            lax.fori_loop(1, 16, piece, 0)

        def part_to(q, _):
            remote(
                xb_ref.at[quarter(q)], pr_ref.at[z, quarter(q)], qs, qr.at[z, q], y, q * 4 + z
            ).start()
            return 0

        @pl.when(y == 0)
        def _():
            pr_ref[pl.ds(z, 1), 0:64] = xb_ref[0:64, :].reshape(1, 64, CB)
            lax.fori_loop(1, 4, part_to, 0)

        @pl.when(y != 0)
        def _():
            lax.fori_loop(0, 4, part_to, 0)

        for o in range(1, 4):
            remote(xb_ref, xb_ref, bs.at[o - 1], br, o, c).start()

    mine = 4 * r + y

    @pl.when(z == 0)
    def _():
        @pl.when(mine != 0)
        def _():
            remote(pv_ref.at[sixteenth(mine)], pv_ref.at[sixteenth(mine)], vs.at[0], vr.at[0], r, c).wait_recv()

        for o in range(1, 4):
            remote(
                pv_ref.at[sixteenth(mine)], pv_ref.at[sixteenth(mine)], vt.at[o - 1], vr.at[0], r, y * 4 + o
            ).start()

    @pl.when(z != 0)
    def _():
        remote(pv_ref.at[sixteenth(mine)], pv_ref.at[sixteenth(mine)], vs.at[0], vr.at[0], r, c).wait_recv()

    def plane(o, _):
        t = lax.rem(mine + o, 16)
        remote(
            pv_ref.at[sixteenth(mine)], pv_ref.at[sixteenth(mine)], vs.at[1], vr.at[1],
            t // 4, (t % 4) * 4 + z,
        ).start()
        return 0

    lax.fori_loop(1, 16, plane, 0)

    @pl.when(jnp.logical_or(r != 0, me >= 4))
    def _():
        remote(pr_ref.at[z, quarter(y)], pr_ref.at[z, quarter(y)], qs, qr.at[z, y], r, c).wait_recv()

    def to_y(zz):
        for o in range(1, 4):
            remote(
                pr_ref.at[zz, quarter(y)], pr_ref.at[zz, quarter(y)], ds.at[2], qr.at[zz, y],
                r, lax.rem(y + o, 4) * 4 + z,
            ).start()

    for o in range(1, 4):
        remote(
            pr_ref.at[z, quarter(y)], pr_ref.at[z, quarter(y)], ds.at[1], qr.at[z, y],
            r, y * 4 + lax.rem(z + o, 4),
        ).start()
    to_y(z)
    for o in range(1, 4):
        zz = lax.rem(z + o, 4)
        remote(pr_ref.at[zz, quarter(y)], pr_ref.at[zz, quarter(y)], qs, qr.at[zz, y], r, c).wait_recv()
        to_y(zz)

    remote(pv_ref.at[0:240], pv_ref.at[0:240], vs.at[1], vr.at[1], r, c).wait_recv()
    factorize(e_ref, pv_ref[...])
    inv = e_ref[:, PW:]

    remote(x_ref.at[pl.ds(0, n - 1)], y_ref.at[pl.ds(0, n - 1)], xs, xr, r, c).wait_recv()

    @pl.when(c != 0)
    def _():
        placed = []
        for k in range(2):
            src = jnp.concatenate(
                [y_ref[s * COLS : (s + 1) * COLS, k].reshape(COLS * CAPC, CAPR) for s in range(ROWS)],
                axis=1,
            )
            placed.append([dot_nn(cpl[k], part).astype(BF16) for part in parts3(src)])
        for s in range(4):
            rows = slice(s * 256, (s + 1) * 256)
            total = f_ref[rows, :]
            for k in range(2):
                rpl = onehot(PW, row_of[k] - s * 256)
                for w in placed[k]:
                    total = total + dot_nt(rpl, w)
            f_ref[rows, :] = total

    @pl.when(r != 0)
    def _():
        remote(xb_ref, xb_ref, bs.at[0], br, r, c).wait_recv()

    for zz in range(4):
        for o in range(1, 4):
            yy = lax.rem(y + o, 4)
            remote(
                pr_ref.at[zz, quarter(yy)], pr_ref.at[zz, quarter(yy)], qs, qr.at[zz, yy], r, c
            ).wait_recv()

    @pl.when(c == 0)
    def _():
        for s in range(4):
            o_ref[s * 256 : (s + 1) * 256, :] = lax.dot_general(
                pr_ref[s], inv, (((0,), (1,)), ((), ())), preferred_element_type=F32,
                precision=lax.Precision.HIGHEST,
            )

        @pl.when(r == 0)
        def _():
            o_ref[:PW, :] = e_ref[:, :PW].T

    @pl.when(c != 0)
    def _():
        right = dot3(dot_nn, inv, xb_ref[...])
        for s in range(4):
            rows = slice(s * 256, (s + 1) * 256)
            left = dot3(dot_nn, inv, pr_ref[s])
            o_ref[rows, :] = f_ref[rows, :] - dot3(dot_tn, left, right)

        @pl.when(r == 0)
        def _():
            o_ref[:PW, :] = jnp.zeros((PW, CB), F32)

    remote(x_ref.at[pl.ds(0, n - 1)], y_ref.at[pl.ds(0, n - 1)], xs, xr, r, c).wait_send()
    remote(pv_ref.at[0:240], pv_ref.at[0:240], vs.at[1], vr.at[1], r, c).wait_send()
    remote(pr_ref.at[0, 0:192], pr_ref.at[0, 0:192], ds.at[1], br, r, c).wait_send()
    remote(pr_ref.at[0:3], pr_ref.at[0:3], ds.at[2], br, r, c).wait_send()

    @pl.when(z == 0)
    def _():
        for o in range(1, 4):
            remote(pv_ref.at[0:16], pv_ref.at[0:16], vt.at[o - 1], br, r, c).wait_send()

    @pl.when(r != 0)
    def _():
        remote(xp_ref, yp_ref.at[pl.ds(0, COLS)], ps, prs, r, c).wait_send()

    @pl.when(r == 0)
    def _():
        remote(xp_ref.at[0:15], yp_ref.at[0:15], ps, prs, r, c).wait_send()

        @pl.when(y == 0)
        def _():
            remote(xb_ref.at[0:192], xb_ref.at[0:192], qs, br, r, c).wait_send()

        @pl.when(y != 0)
        def _():
            remote(xb_ref, xb_ref, qs, br, r, c).wait_send()

        @pl.when(c == 0)
        def _():
            remote(xb_ref.at[0:240], xb_ref.at[0:240], vs.at[0], br, r, c).wait_send()

        for o in range(1, 4):
            remote(xb_ref, xb_ref, bs.at[o - 1], br, r, c).wait_send()


def shape(*s):
    return jax.ShapeDtypeStruct(s, F32)


def per_device(front_matrix, child_updates, child_map):
    dma = pltpu.SemaphoreType.DMA
    out = pl.pallas_call(
        kernel,
        out_shape=shape(RB, CB),
        in_specs=[
            pl.BlockSpec(memory_space=pltpu.VMEM),
            pl.BlockSpec(memory_space=pl.ANY),
            pl.BlockSpec(memory_space=pl.ANY),
        ],
        out_specs=pl.BlockSpec(memory_space=pltpu.VMEM),
        scratch_shapes=[
            pltpu.VMEM((UR, UCB), F32),
            pltpu.VMEM((UR, UCB), F32),
            pltpu.VMEM((2, ROWS * UR), jnp.int32),
            pltpu.VMEM((RB, CB), F32),
            pltpu.VMEM((ROWS * COLS, 2, CAPC, CAPR), F32),
            pltpu.VMEM((ROWS * COLS, 2, CAPC, CAPR), F32),
            pltpu.VMEM((COLS, CAPC, 2 * CAPP), F32),
            pltpu.VMEM((ROWS * COLS, CAPC, 2 * CAPP), F32),
            pltpu.VMEM((PW, CB), F32),
            pltpu.VMEM((4, PW, CB), F32),
            pltpu.VMEM((PW, CB), F32),
            pltpu.VMEM((PW, 2 * PW), F32),
            dma((2,)), dma((2,)), dma((2,)),
            dma, dma, dma, dma, dma((3,)), dma, dma, dma((4, 4)), dma((3,)), dma((2,)), dma((2,)),
            dma((3,)),
        ],
        compiler_params=pltpu.CompilerParams(
            vmem_limit_bytes=VMEM_LIMIT, collective_id=1, has_side_effects=True
        ),
    )(child_map[0], child_updates[0], front_matrix[0])
    return out[None]


def solution(mesh):
    in_specs = (P("front", "row", "col"), P("front", None, "row", "col"), P("front", None, None))
    return jax.shard_map(
        per_device, mesh=mesh, in_specs=in_specs, out_specs=P("front", "row", "col"), check_vma=False
    )
```

time: 79 us -> 68.2 us (0.86); the launches traced: 78.8 us -> 66.9 us
  Pallas kernels: 75 us -> 62.9 us
  local copies, waits for them, and re-layouts: 1.93 us -> 3.95 us
  waiting for transfers between devices: 1.04 us -> 0 us
    pallas_call x3 -> x1, Pallas kernels: 75 us -> 62.9 us  [per_device(): pl.pallas_call(kernel, out_shape=shape(RB, CB), in_specs=[pl.BlockSpec(me...]
    unnamed x2 -> x7, local copies, waits for them, and re-layouts: 0.01 us -> 3.95 us
    squeeze x1 -> x0, local copies, waits for them, and re-layouts: 1.07 us -> none  [per_device(): u1 = lax.ppermute(child_updates[0, 1], 'front', pairs)]
    ppermute x2 -> x0, waiting for transfers between devices: 1.04 us -> none  [the longest x1 1.04 us: per_device(): u1 = lax.ppermute(child_updates[0, 1], 'front', pairs)]
    another operation x1 -> x0, local copies, waits for them, and re-layouts: 0.84 us -> none  [per_device(): maps = jnp.stack([child_map[0, 0], m1])]
  transfers between devices with their start and end apart: 2 -> 0, of which waited for: 1 -> 0; matrix products, arithmetic and copies ran while one was open for 1% -> 0% of each run, Pallas kernels for 0% -> 0%
where the time goes in v3:
time: 68.2 us; the launch traced here: 66.9 us
  Pallas kernels  62.9 us (92%)
  local copies, waits for them, and re-layouts  3.95 us (6%)
    pallas_call x1, Pallas kernels, per_device(): pl.pallas_call(kernel, out_shape=shape(RB, CB), in_specs=[pl.BlockSpec(me...  62.9 us
    unnamed x7, local copies, waits for them, and re-layouts  3.95 us

profile of v3, /device:TPU:12, one launch (start us, length us, event | category | flops | bytes accessed | tf_op | source)
XLA Modules:
  0.0 66.9 jit_solution(908027893738423813)
XLA Ops:
  0.0 0.0 copy-start
  0.0 1.2 %copy-done = f32[1,1024,256]{2,1,0:T(8,128)S(1)} copy-done((f32[1,1024,256]{2,1,0:T(8,128)S(1)}, f32[1,1024,256]{2,1,0:T(8,128)}, u32[]{:S(2)}) %copy-start) | copy-done | bytes 1048600
  1.2 0.0 copy-start.1
  1.2 1.0 %copy-done.1 = f32[1,2,512,128]{3,2,1,0:T(8,128)S(1)} copy-done((f32[1,2,512,128]{3,2,1,0:T(8,128)S(1)}, f32[1,2,512,128]{3,2,1,0:T(8,128)}, u32[]{:S(2)}) %copy-start.1) | copy-done | bytes 524312
  2.3 0.0 copy-start.2
  2.3 0.7 %copy-done.2 = s32[1,2,2048]{2,1,0:T(2,128)S(1)} copy-done((s32[1,2,2048]{2,1,0:T(2,128)S(1)}, s32[1,2,2048]{2,1,0:T(2,128)}, u32[]{:S(2)}) %copy-start.2) | copy-done | bytes 16408
  3.0 62.9 %shard_map.37 = f32[1024,256]{1,0:T(8,128)S(1)} custom-call(s32[2,2048]{1,0:T(2,128)S(1)} %bitcast.7, f32[2,512,128]{2,1,0:T(8,128)S(1)} %bitcast.6, f32[1024,256]{1,0:T(8,128)S(1)} %bitcast.5), custom_call_target="tpu_custom_call" | custom-call | tf_op jit(solution)/shard_map/pallas_call | solution.py:469
  65.9 1.0 %copy.5 = f32[1,1024,256]{2,1,0:T(8,128)} copy(f32[1,1024,256]{2,1,0:T(8,128)S(1)} %bitcast.4) | data formatting | bytes 2097152
Async XLA Ops:
  0.0 1.2 %copy-start = (f32[1,1024,256]{2,1,0:T(8,128)S(1)}, f32[1,1024,256]{2,1,0:T(8,128)}, u32[]{:S(2)}) copy-start(f32[1,1024,256]{2,1,0:T(8,128)} %param.3) | copy-start | bytes 3145732
  1.2 1.0 %copy-start.1 = (f32[1,2,512,128]{3,2,1,0:T(8,128)S(1)}, f32[1,2,512,128]{3,2,1,0:T(8,128)}, u32[]{:S(2)}) copy-start(f32[1,2,512,128]{3,2,1,0:T(8,128)} %param.4) | copy-start | bytes 1572868
  2.3 0.7 %copy-start.2 = (s32[1,2,2048]{2,1,0:T(2,128)S(1)}, s32[1,2,2048]{2,1,0:T(2,128)}, u32[]{:S(2)}) copy-start(s32[1,2,2048]{2,1,0:T(2,128)} %param.5) | copy-start | bytes 49156

commit v4 on v3

--- a/solution.py
+++ b/solution.py
@@ -21,7 +21,7 @@
 MESH = pl.DeviceIdType.MESH
 F32 = jnp.float32
 BF16 = jnp.bfloat16
-VMEM_LIMIT = 48 * 1024 * 1024
+VMEM_LIMIT = 60 * 1024 * 1024
 
 
 def parts3(x):
@@ -75,11 +75,15 @@
     return dest * cap + rank.astype(jnp.int32)
 
 
-def factorize(m_ref, pv):
+def set_up(m_ref, pv):
     n = PW
     m_ref[:, :n] = pv
     m_ref[:, n:] = (iota((n, n), 0) == iota((n, n), 1)).astype(F32)
-    for b0 in range(0, n, OB):
+
+
+def eliminate(m_ref, begin, end):
+    n = PW
+    for b0 in range(begin, end, OB):
         lo = (b0 // 128) * 128
         hi = n + ((b0 + OB - 1) // 128) * 128 + 128
         R = [m_ref[b0 + 8 * i : b0 + 8 * i + 8, lo:hi] for i in range(OB // 8)]
@@ -148,6 +152,26 @@
         return 0
 
     lax.fori_loop(1, n, greet, 0)
+    load_u.wait()
+    columns = []
+
+    def pack_columns(m, values):
+        mc = m[:, pl.ds(pl.multiple_of(c * UCB, UCB), UCB)]
+        cp = onehot(COLS * CAPC, ranked_slot(mc // CB, COLS, CAPC))
+        columns.append([dot_nt(cp, part).astype(BF16) for part in parts3(values)])
+
+    def pack_panel(k, m, panel):
+        mr = m[:, pl.ds(pl.multiple_of(r * UR, UR), UR)]
+        first = mr < PW
+        place = ranked_slot(jnp.where(first, 0, 1), 8, 0) + CAPP * k
+        pp = onehot(2 * CAPP, jnp.where(first, place, -1))
+        for t in columns[k]:
+            piece = dot_nt(t, pp)
+            panel = piece if panel is None else panel + piece
+        return panel
+
+    pack_columns(m_ref.at[0:1], u0_ref[...])
+    panel = pack_panel(0, m_ref.at[0:1], None)
     pl.semaphore_wait(barrier, n)
 
     def remote(src, dst, s_sem, r_sem, row, col):
@@ -158,6 +182,9 @@
 
     def quarter(i):
         return pl.ds(pl.multiple_of(i * 64, 64), 64)
+
+    def half(i):
+        return pl.ds(i * 128, 128)
 
     def sixteenth(i):
         return pl.ds(pl.multiple_of(i * 16, 16), 16)
@@ -176,25 +203,10 @@
     def maps(k):
         return m_ref if k == 0 else mp_ref
 
-    panel = None
-    columns = []
-    for k in range(2):
-        if k == 0:
-            load_u.wait()
-        else:
-            swap_m.wait()
-            swap_u.wait()
-        mr = maps(k)[k : k + 1, pl.ds(pl.multiple_of(r * UR, UR), UR)]
-        mc = maps(k)[k : k + 1, pl.ds(pl.multiple_of(c * UCB, UCB), UCB)]
-        cp = onehot(COLS * CAPC, ranked_slot(mc // CB, COLS, CAPC))
-        first = mr < PW
-        place = ranked_slot(jnp.where(first, 0, 1), 8, 0) + CAPP * k
-        pp = onehot(2 * CAPP, jnp.where(first, place, -1))
-        values = u0_ref[...] if k == 0 else u1_ref[...]
-        columns.append([dot_nt(cp, part).astype(BF16) for part in parts3(values)])
-        for t in columns[k]:
-            piece = dot_nt(t, pp)
-            panel = piece if panel is None else panel + piece
+    swap_m.wait()
+    swap_u.wait()
+    pack_columns(mp_ref.at[1:2], u1_ref[...])
+    panel = pack_panel(1, mp_ref.at[1:2], panel)
     xp_ref[...] = panel.reshape(COLS, CAPC, 2 * CAPP)
 
     def send_panel(o, _):
@@ -222,10 +234,14 @@
 
     def send_bulk(o, _):
         t = lax.rem(me + o, n)
-        remote(x_ref.at[t], y_ref.at[me], xs, xr, t // COLS, t % COLS).start()
+
+        @pl.when(t % COLS != 0)
+        def _():
+            remote(x_ref.at[t], y_ref.at[me], xs, xr, t // COLS, t % COLS).start()
+
         return 0
 
-    lax.fori_loop(1, n, send_bulk, 0)
+    lax.fori_loop(1, 64, send_bulk, 0)
     y_ref[pl.ds(me, 1)] = x_ref[pl.ds(me, 1)]
 
     mi = jnp.concatenate(
@@ -315,8 +331,13 @@
         def _():
             lax.fori_loop(0, 4, part_to, 0)
 
-        for o in range(1, 4):
-            remote(xb_ref, xb_ref, bs.at[o - 1], br, o, c).start()
+        def half_to(i, h, row):
+            remote(xb_ref.at[half(h)], xb_ref.at[half(h)], bs.at[i], br.at[h], row, c).start()
+
+        half_to(0, 0, 1)
+        half_to(1, 1, 3)
+        half_to(2, 1, 1)
+        half_to(3, 0, 3)
 
     mine = 4 * r + y
 
@@ -367,14 +388,24 @@
         remote(pr_ref.at[zz, quarter(y)], pr_ref.at[zz, quarter(y)], qs, qr.at[zz, y], r, c).wait_recv()
         to_y(zz)
 
+    @pl.when(r == 1)
+    def _():
+        remote(xb_ref.at[half(0)], xb_ref.at[half(0)], bs.at[0], br.at[0], r, c).wait_recv()
+        remote(xb_ref.at[half(0)], xb_ref.at[half(0)], bs.at[0], br.at[0], 2, c).start()
+
+    @pl.when(r == 3)
+    def _():
+        remote(xb_ref.at[half(1)], xb_ref.at[half(1)], bs.at[0], br.at[1], r, c).wait_recv()
+        remote(xb_ref.at[half(1)], xb_ref.at[half(1)], bs.at[0], br.at[1], 2, c).start()
+
     remote(pv_ref.at[0:240], pv_ref.at[0:240], vs.at[1], vr.at[1], r, c).wait_recv()
-    factorize(e_ref, pv_ref[...])
+    set_up(e_ref, pv_ref[...])
+    eliminate(e_ref, 0, PW)
     inv = e_ref[:, PW:]
 
-    remote(x_ref.at[pl.ds(0, n - 1)], y_ref.at[pl.ds(0, n - 1)], xs, xr, r, c).wait_recv()
-
     @pl.when(c != 0)
     def _():
+        remote(x_ref.at[pl.ds(0, n - 1)], y_ref.at[pl.ds(0, n - 1)], xs, xr, r, c).wait_recv()
         placed = []
         for k in range(2):
             src = jnp.concatenate(
@@ -391,9 +422,13 @@
                     total = total + dot_nt(rpl, w)
             f_ref[rows, :] = total
 
-    @pl.when(r != 0)
-    def _():
-        remote(xb_ref, xb_ref, bs.at[0], br, r, c).wait_recv()
+    @pl.when(jnp.logical_or(r == 2, r == 3))
+    def _():
+        remote(xb_ref.at[half(0)], xb_ref.at[half(0)], bs.at[0], br.at[0], r, c).wait_recv()
+
+    @pl.when(jnp.logical_or(r == 1, r == 2))
+    def _():
+        remote(xb_ref.at[half(1)], xb_ref.at[half(1)], bs.at[0], br.at[1], r, c).wait_recv()
 
     for zz in range(4):
         for o in range(1, 4):
@@ -422,19 +457,22 @@
             left = dot3(dot_nn, inv, pr_ref[s])
             o_ref[rows, :] = f_ref[rows, :] - dot3(dot_tn, left, right)
 
-        @pl.when(r == 0)
-        def _():
-            o_ref[:PW, :] = jnp.zeros((PW, CB), F32)
-
-    remote(x_ref.at[pl.ds(0, n - 1)], y_ref.at[pl.ds(0, n - 1)], xs, xr, r, c).wait_send()
+    @pl.when(c == 0)
+    def _():
+        remote(x_ref.at[0:60], y_ref.at[0:60], xs, xr, r, c).wait_send()
+
+    @pl.when(c != 0)
+    def _():
+        remote(x_ref.at[0:59], y_ref.at[0:59], xs, xr, r, c).wait_send()
+
     remote(pv_ref.at[0:240], pv_ref.at[0:240], vs.at[1], vr.at[1], r, c).wait_send()
-    remote(pr_ref.at[0, 0:192], pr_ref.at[0, 0:192], ds.at[1], br, r, c).wait_send()
-    remote(pr_ref.at[0:3], pr_ref.at[0:3], ds.at[2], br, r, c).wait_send()
+    remote(pr_ref.at[0, 0:192], pr_ref.at[0, 0:192], ds.at[1], br.at[0], r, c).wait_send()
+    remote(pr_ref.at[0:3], pr_ref.at[0:3], ds.at[2], br.at[0], r, c).wait_send()
 
     @pl.when(z == 0)
     def _():
         for o in range(1, 4):
-            remote(pv_ref.at[0:16], pv_ref.at[0:16], vt.at[o - 1], br, r, c).wait_send()
+            remote(pv_ref.at[0:16], pv_ref.at[0:16], vt.at[o - 1], br.at[0], r, c).wait_send()
 
     @pl.when(r != 0)
     def _():
@@ -446,18 +484,22 @@
 
         @pl.when(y == 0)
         def _():
-            remote(xb_ref.at[0:192], xb_ref.at[0:192], qs, br, r, c).wait_send()
+            remote(xb_ref.at[0:192], xb_ref.at[0:192], qs, br.at[0], r, c).wait_send()
 
         @pl.when(y != 0)
         def _():
-            remote(xb_ref, xb_ref, qs, br, r, c).wait_send()
+            remote(xb_ref, xb_ref, qs, br.at[0], r, c).wait_send()
 
         @pl.when(c == 0)
         def _():
-            remote(xb_ref.at[0:240], xb_ref.at[0:240], vs.at[0], br, r, c).wait_send()
-
-        for o in range(1, 4):
-            remote(xb_ref, xb_ref, bs.at[o - 1], br, r, c).wait_send()
+            remote(xb_ref.at[0:240], xb_ref.at[0:240], vs.at[0], br.at[0], r, c).wait_send()
+
+        for i in range(4):
+            remote(xb_ref.at[0:128], xb_ref.at[0:128], bs.at[i], br.at[0], r, c).wait_send()
+
+    @pl.when(jnp.logical_or(r == 1, r == 3))
+    def _():
+        remote(xb_ref.at[0:128], xb_ref.at[0:128], bs.at[0], br.at[0], r, c).wait_send()
 
 
 def shape(*s):
@@ -489,14 +531,16 @@
             pltpu.VMEM((PW, CB), F32),
             pltpu.VMEM((PW, 2 * PW), F32),
             dma((2,)), dma((2,)), dma((2,)),
-            dma, dma, dma, dma, dma((3,)), dma, dma, dma((4, 4)), dma((3,)), dma((2,)), dma((2,)),
+            dma, dma, dma, dma, dma((4,)), dma((2,)), dma, dma((4, 4)), dma((3,)), dma((2,)), dma((2,)),
             dma((3,)),
         ],
         compiler_params=pltpu.CompilerParams(
             vmem_limit_bytes=VMEM_LIMIT, collective_id=1, has_side_effects=True
         ),
     )(child_map[0], child_updates[0], front_matrix[0])
-    return out[None]
+    zero = jnp.logical_and(lax.axis_index("row") == 0, lax.axis_index("col") > 0)
+    kept = jnp.logical_or(iota((RB, CB), 0) >= PW, jnp.logical_not(zero))
+    return jnp.where(kept, out, 0.0)[None]
 
 
 def solution(mesh):

time: 68.2 us -> 62.4 us (0.915); the launches traced: 66.9 us -> 62.2 us
  local copies, waits for them, and re-layouts: 3.95 us -> 0 us
  Pallas kernels: 62.9 us -> 59.8 us
  other arithmetic: 0 us -> 2.41 us
    unnamed x7 -> x0, local copies, waits for them, and re-layouts: 3.95 us -> none
    pallas_call x1, Pallas kernels: 62.9 us -> 59.8 us  [per_device(): pl.pallas_call(kernel, out_shape=shape(RB, CB), in_specs=[pl.BlockSpec(me...]
    broadcast_in_dim x0 -> x1, other arithmetic: none -> 2.4 us  [per_device(): return jnp.where(kept, out, 0.0)[None]]
where the time goes in v4:
time: 62.4 us; the launch traced here: 62.2 us
  Pallas kernels  59.8 us (96%)
  other arithmetic  2.41 us (4%)
    pallas_call x1, Pallas kernels, per_device(): pl.pallas_call(kernel, out_shape=shape(RB, CB), in_specs=[pl.BlockSpec(me...  59.8 us
    broadcast_in_dim x1, other arithmetic, per_device(): return jnp.where(kept, out, 0.0)[None]  2.4 us

profile of v4, /device:TPU:12, one launch (start us, length us, event | category | flops | bytes accessed | tf_op | source)
XLA Modules:
  0.0 62.2 jit_solution(11383894905207249436)
XLA Ops:
  0.0 59.8 %shard_map.37 = f32[1024,256]{1,0:T(8,128)} custom-call(s32[2,2048]{1,0:T(2,128)} %bitcast.7, f32[2,512,128]{2,1,0:T(8,128)} %bitcast.6, f32[1024,256]{1,0:T(8,128)} %bitcast.5), custom_call_target="tpu_custom_call" | custom-call | tf_op jit(solution)/shard_map/pallas_call | solution.py:511
  59.8 2.4 %select_bitcast_fusion = f32[1,1024,256]{2,1,0:T(8,128)} fusion(f32[1024,256]{1,0:T(8,128)} %shard_map.37, pred[1024]{0:T(1024)(128)(4,1)S(1)} %fusion), kind=kLoop, calls=%fused_computation | loop fusion | flops 262144 | bytes 2098176 | tf_op jit(solution)/shard_map/broadcast_in_dim | solution.py:543
  (1 shorter events, 0.0 us)

commit v5 on v4

--- a/solution.py
+++ b/solution.py
@@ -21,7 +21,7 @@
 MESH = pl.DeviceIdType.MESH
 F32 = jnp.float32
 BF16 = jnp.bfloat16
-VMEM_LIMIT = 60 * 1024 * 1024
+VMEM_LIMIT = 48 * 1024 * 1024
 
 
 def parts3(x):
@@ -123,9 +123,9 @@
 
 
 def kernel(
-    m_ref, u_ref, f_hbm, o_ref,
-    u0_ref, u1_ref, mp_ref, f_ref, x_ref, y_ref, xp_ref, yp_ref, xb_ref, pr_ref, pv_ref, e_ref,
-    lo_sem, us, ur, xs, xr, ps, prs, bs, br, qs, qr, ds, vs, vr, vt,
+    m_ref, u_ref, f_ref, o_ref,
+    u1_ref, mp_ref, a_ref, x_ref, y_ref, xp_ref, yp_ref, xb_ref, pr_ref, pv_ref, e_ref,
+    us, ur, xs, xr, ps, prs, bs, br, qs, qr, ds, vs, vr, vt,
 ):
     f = lax.axis_index("front")
     r = lax.axis_index("row")
@@ -135,11 +135,6 @@
     me = r * COLS + c
     n = ROWS * COLS
     other = f + 1 - 2 * (f % 2)
-    load_u = pltpu.make_async_copy(u_ref.at[0], u0_ref, lo_sem.at[0])
-    load_u.start()
-    load_f = pltpu.make_async_copy(f_hbm, f_ref, lo_sem.at[1])
-    load_f.start()
-
     barrier = pltpu.get_barrier_semaphore()
     partner = {"front": other, "row": r, "col": c}
     pl.semaphore_signal(barrier, inc=1, device_id=partner, device_id_type=MESH)
@@ -152,7 +147,6 @@
         return 0
 
     lax.fori_loop(1, n, greet, 0)
-    load_u.wait()
     columns = []
 
     def pack_columns(m, values):
@@ -170,8 +164,21 @@
             panel = piece if panel is None else panel + piece
         return panel
 
-    pack_columns(m_ref.at[0:1], u0_ref[...])
+    def pack_rows(k, m):
+        mr = m[:, pl.ds(pl.multiple_of(r * UR, UR), UR)]
+        rp = onehot(UR, ranked_slot(mr // RB, 8, CAPR))
+        x = None
+        for t in columns[k]:
+            piece = dot_nt(t, rp)
+            x = piece if x is None else x + piece
+        for dst in range(ROWS):
+            x_ref[dst * COLS : (dst + 1) * COLS, k] = x[
+                :, dst * CAPR : (dst + 1) * CAPR
+            ].reshape(COLS, CAPC, CAPR)
+
+    pack_columns(m_ref.at[0:1], u_ref[0])
     panel = pack_panel(0, m_ref.at[0:1], None)
+    pack_rows(0, m_ref.at[0:1])
     pl.semaphore_wait(barrier, n)
 
     def remote(src, dst, s_sem, r_sem, row, col):
@@ -203,6 +210,17 @@
     def maps(k):
         return m_ref if k == 0 else mp_ref
 
+    def send_child(k, o):
+        t = lax.rem(me + o, n)
+
+        @pl.when(t % COLS != 0)
+        def _():
+            remote(x_ref.at[t, k], y_ref.at[me, k], xs, xr, t // COLS, t % COLS).start()
+
+        return 0
+
+    lax.fori_loop(1, 25, lambda o, _: send_child(0, o), 0)
+
     swap_m.wait()
     swap_u.wait()
     pack_columns(mp_ref.at[1:2], u1_ref[...])
@@ -220,17 +238,7 @@
     def _():
         remote(xp_ref.at[c], yp_ref.at[me], ps, prs, 0, c).start()
 
-    for k in range(2):
-        mr = maps(k)[k : k + 1, pl.ds(pl.multiple_of(r * UR, UR), UR)]
-        rp = onehot(UR, ranked_slot(mr // RB, 8, CAPR))
-        x = None
-        for t in columns[k]:
-            piece = dot_nt(t, rp)
-            x = piece if x is None else x + piece
-        for dst in range(ROWS):
-            x_ref[dst * COLS : (dst + 1) * COLS, k] = x[
-                :, dst * CAPR : (dst + 1) * CAPR
-            ].reshape(COLS, CAPC, CAPR)
+    pack_rows(1, mp_ref.at[1:2])
 
     def send_bulk(o, _):
         t = lax.rem(me + o, n)
@@ -241,7 +249,8 @@
 
         return 0
 
-    lax.fori_loop(1, 64, send_bulk, 0)
+    lax.fori_loop(25, n, send_bulk, 0)
+    lax.fori_loop(1, 25, lambda o, _: send_child(1, o), 0)
     y_ref[pl.ds(me, 1)] = x_ref[pl.ds(me, 1)]
 
     mi = jnp.concatenate(
@@ -285,8 +294,6 @@
         col_of.append(got[0:1, :].astype(jnp.int32))
     cpl = [onehot(CB, col_of[k]) for k in range(2)]
 
-    load_f.wait()
-
     @pl.when(r == 0)
     def _():
         yp_ref[pl.ds(me, 1)] = xp_ref[pl.ds(c, 1)]
@@ -412,7 +419,7 @@
                 [y_ref[s * COLS : (s + 1) * COLS, k].reshape(COLS * CAPC, CAPR) for s in range(ROWS)],
                 axis=1,
             )
-            placed.append([dot_nn(cpl[k], part).astype(BF16) for part in parts3(src)])
+            placed.append([dot_nn(cpl[k], part).astype(BF16) for part in split2(src)])
         for s in range(4):
             rows = slice(s * 256, (s + 1) * 256)
             total = f_ref[rows, :]
@@ -420,7 +427,7 @@
                 rpl = onehot(PW, row_of[k] - s * 256)
                 for w in placed[k]:
                     total = total + dot_nt(rpl, w)
-            f_ref[rows, :] = total
+            a_ref[rows, :] = total
 
     @pl.when(jnp.logical_or(r == 2, r == 3))
     def _():
@@ -455,7 +462,7 @@
         for s in range(4):
             rows = slice(s * 256, (s + 1) * 256)
             left = dot3(dot_nn, inv, pr_ref[s])
-            o_ref[rows, :] = f_ref[rows, :] - dot3(dot_tn, left, right)
+            o_ref[rows, :] = a_ref[rows, :] - dot3(dot_tn, left, right)
 
     @pl.when(c == 0)
     def _():
@@ -513,12 +520,11 @@
         out_shape=shape(RB, CB),
         in_specs=[
             pl.BlockSpec(memory_space=pltpu.VMEM),
-            pl.BlockSpec(memory_space=pl.ANY),
-            pl.BlockSpec(memory_space=pl.ANY),
+            pl.BlockSpec(memory_space=pltpu.VMEM),
+            pl.BlockSpec(memory_space=pltpu.VMEM),
         ],
         out_specs=pl.BlockSpec(memory_space=pltpu.VMEM),
         scratch_shapes=[
-            pltpu.VMEM((UR, UCB), F32),
             pltpu.VMEM((UR, UCB), F32),
             pltpu.VMEM((2, ROWS * UR), jnp.int32),
             pltpu.VMEM((RB, CB), F32),
@@ -530,7 +536,7 @@
             pltpu.VMEM((4, PW, CB), F32),
             pltpu.VMEM((PW, CB), F32),
             pltpu.VMEM((PW, 2 * PW), F32),
-            dma((2,)), dma((2,)), dma((2,)),
+            dma((2,)), dma((2,)),
             dma, dma, dma, dma, dma((4,)), dma((2,)), dma, dma((4, 4)), dma((3,)), dma((2,)), dma((2,)),
             dma((3,)),
         ],

time: 62.4 us -> 60.1 us (0.963)
  Pallas kernels: 59.8 us -> 55.2 us
  local copies, waits for them, and re-layouts: 0 us -> 2.97 us
  other arithmetic: 2.41 us -> 1.18 us
    pallas_call x1, Pallas kernels: 59.8 us -> 55.2 us  [per_device(): pl.pallas_call(kernel, out_shape=shape(RB, CB), in_specs=[pl.BlockSpec(me...]
    unnamed x0 -> x6, local copies, waits for them, and re-layouts: none -> 2.97 us
    broadcast_in_dim x1, other arithmetic: 2.4 us -> 1.17 us  [per_device(): return jnp.where(kept, out, 0.0)[None]]
where the time goes in v5:
time: 60.1 us; the launch traced here: 59.4 us
  Pallas kernels  55.2 us (92%)
  local copies, waits for them, and re-layouts  2.97 us (5%)
  other arithmetic  1.18 us (2%)
    pallas_call x1, Pallas kernels, per_device(): pl.pallas_call(kernel, out_shape=shape(RB, CB), in_specs=[pl.BlockSpec(me...  55.2 us
    unnamed x6, local copies, waits for them, and re-layouts  2.97 us

profile of v5, /device:TPU:12, one launch (start us, length us, event | category | flops | bytes accessed | tf_op | source)
XLA Modules:
  0.0 59.4 jit_solution(7873134082528362259)
XLA Ops:
  0.0 0.0 copy-start.2
  0.0 0.7 %copy-done.2 = s32[1,2,2048]{2,1,0:T(2,128)S(1)} copy-done((s32[1,2,2048]{2,1,0:T(2,128)S(1)}, s32[1,2,2048]{2,1,0:T(2,128)}, u32[]{:S(2)}) %copy-start.2) | copy-done | bytes 16408
  0.7 0.0 copy-start
  0.7 1.2 %copy-done = f32[1,1024,256]{2,1,0:T(8,128)S(1)} copy-done((f32[1,1024,256]{2,1,0:T(8,128)S(1)}, f32[1,1024,256]{2,1,0:T(8,128)}, u32[]{:S(2)}) %copy-start) | copy-done | bytes 1048600
  1.9 0.0 copy-start.1
  1.9 1.0 %copy-done.1 = f32[1,2,512,128]{3,2,1,0:T(8,128)S(1)} copy-done((f32[1,2,512,128]{3,2,1,0:T(8,128)S(1)}, f32[1,2,512,128]{3,2,1,0:T(8,128)}, u32[]{:S(2)}) %copy-start.1) | copy-done | bytes 524312
  3.0 55.2 %shard_map.37 = f32[1024,256]{1,0:T(8,128)S(1)} custom-call(s32[2,2048]{1,0:T(2,128)S(1)} %bitcast.7, f32[2,512,128]{2,1,0:T(8,128)S(1)} %bitcast.6, f32[1024,256]{1,0:T(8,128)S(1)} %bitcast.5), custom_call_target="tpu_custom_call" | custom-call | tf_op jit(solution)/shard_map/pallas_call | solution.py:518
  58.2 1.2 %select_bitcast_fusion = f32[1,1024,256]{2,1,0:T(8,128)} fusion(f32[1024,256]{1,0:T(8,128)S(1)} %shard_map.37, pred[1024]{0:T(1024)(128)(4,1)S(1)} %fusion), kind=kLoop, calls=%fused_computation | loop fusion | flops 262144 | bytes 2098176 | tf_op jit(solution)/shard_map/broadcast_in_dim | solution.py:549
  (1 shorter events, 0.0 us)
Async XLA Ops:
  0.0 0.7 %copy-start.2 = (s32[1,2,2048]{2,1,0:T(2,128)S(1)}, s32[1,2,2048]{2,1,0:T(2,128)}, u32[]{:S(2)}) copy-start(s32[1,2,2048]{2,1,0:T(2,128)} %param.5) | copy-start | bytes 49156
  0.7 1.2 %copy-start = (f32[1,1024,256]{2,1,0:T(8,128)S(1)}, f32[1,1024,256]{2,1,0:T(8,128)}, u32[]{:S(2)}) copy-start(f32[1,1024,256]{2,1,0:T(8,128)} %param.3) | copy-start | bytes 3145732
  1.9 1.0 %copy-start.1 = (f32[1,2,512,128]{3,2,1,0:T(8,128)S(1)}, f32[1,2,512,128]{3,2,1,0:T(8,128)}, u32[]{:S(2)}) copy-start(f32[1,2,512,128]{3,2,1,0:T(8,128)} %param.4) | copy-start | bytes 1572868

commit v6 on v5

--- a/solution.py
+++ b/solution.py
@@ -78,7 +78,6 @@
 def set_up(m_ref, pv):
     n = PW
     m_ref[:, :n] = pv
-    m_ref[:, n:] = (iota((n, n), 0) == iota((n, n), 1)).astype(F32)
 
 
 def eliminate(m_ref, begin, end):
@@ -124,7 +123,7 @@
 
 def kernel(
     m_ref, u_ref, f_ref, o_ref,
-    u1_ref, mp_ref, a_ref, x_ref, y_ref, xp_ref, yp_ref, xb_ref, pr_ref, pv_ref, e_ref,
+    u1_ref, mp_ref, place_ref, a_ref, x_ref, y_ref, xp_ref, yp_ref, xb_ref, pr_ref, pv_ref, e_ref,
     us, ur, xs, xr, ps, prs, bs, br, qs, qr, ds, vs, vr, vt,
 ):
     f = lax.axis_index("front")
@@ -294,6 +293,16 @@
         col_of.append(got[0:1, :].astype(jnp.int32))
     cpl = [onehot(CB, col_of[k]) for k in range(2)]
 
+    def prepare():
+        for k in range(2):
+            for s in range(4):
+                place_ref[k, s * 256 : (s + 1) * 256, :] = onehot(PW, row_of[k] - s * 256)
+        e_ref[:, PW:] = (iota((PW, PW), 0) == iota((PW, PW), 1)).astype(F32)
+
+    @pl.when(r != 0)
+    def _():
+        prepare()
+
     @pl.when(r == 0)
     def _():
         yp_ref[pl.ds(me, 1)] = xp_ref[pl.ds(c, 1)]
@@ -390,8 +399,15 @@
             r, y * 4 + lax.rem(z + o, 4),
         ).start()
     to_y(z)
-    for o in range(1, 4):
-        zz = lax.rem(z + o, 4)
+
+    @pl.when(r == 0)
+    def _():
+        prepare()
+
+    for i in range(3):
+        up = jnp.where(i >= z, i + 1, i)
+        down = jnp.where(3 - i <= z, 2 - i, 3 - i)
+        zz = jnp.where(z < 2, up, down)
         remote(pr_ref.at[zz, quarter(y)], pr_ref.at[zz, quarter(y)], qs, qr.at[zz, y], r, c).wait_recv()
         to_y(zz)
 
@@ -424,7 +440,7 @@
             rows = slice(s * 256, (s + 1) * 256)
             total = f_ref[rows, :]
             for k in range(2):
-                rpl = onehot(PW, row_of[k] - s * 256)
+                rpl = place_ref[k, rows, :]
                 for w in placed[k]:
                     total = total + dot_nt(rpl, w)
             a_ref[rows, :] = total
@@ -527,6 +543,7 @@
         scratch_shapes=[
             pltpu.VMEM((UR, UCB), F32),
             pltpu.VMEM((2, ROWS * UR), jnp.int32),
+            pltpu.VMEM((2, RB, UR), BF16),
             pltpu.VMEM((RB, CB), F32),
             pltpu.VMEM((ROWS * COLS, 2, CAPC, CAPR), F32),
             pltpu.VMEM((ROWS * COLS, 2, CAPC, CAPR), F32),

time: 60.1 us -> 59.9 us (level)
  no operation moved by 1% of the time
where the time goes in v6:
time: 59.9 us; the launch traced here: 59.2 us
  Pallas kernels  55.1 us (92%)
  local copies, waits for them, and re-layouts  2.97 us (5%)
  other arithmetic  1.18 us (2%)
    pallas_call x1, Pallas kernels, per_device(): pl.pallas_call(kernel, out_shape=shape(RB, CB), in_specs=[pl.BlockSpec(me...  55.1 us
    unnamed x6, local copies, waits for them, and re-layouts  2.97 us

profile of v6, /device:TPU:12, one launch (start us, length us, event | category | flops | bytes accessed | tf_op | source)
XLA Modules:
  0.0 59.2 jit_solution(5700442692165171530)
XLA Ops:
  0.0 0.0 copy-start.2
  0.0 0.7 %copy-done.2 = s32[1,2,2048]{2,1,0:T(2,128)S(1)} copy-done((s32[1,2,2048]{2,1,0:T(2,128)S(1)}, s32[1,2,2048]{2,1,0:T(2,128)}, u32[]{:S(2)}) %copy-start.2) | copy-done | bytes 16408
  0.7 0.0 copy-start
  0.7 1.2 %copy-done = f32[1,1024,256]{2,1,0:T(8,128)S(1)} copy-done((f32[1,1024,256]{2,1,0:T(8,128)S(1)}, f32[1,1024,256]{2,1,0:T(8,128)}, u32[]{:S(2)}) %copy-start) | copy-done | bytes 1048600
  1.9 0.0 copy-start.1
  1.9 1.0 %copy-done.1 = f32[1,2,512,128]{3,2,1,0:T(8,128)S(1)} copy-done((f32[1,2,512,128]{3,2,1,0:T(8,128)S(1)}, f32[1,2,512,128]{3,2,1,0:T(8,128)}, u32[]{:S(2)}) %copy-start.1) | copy-done | bytes 524312
  3.0 55.1 %shard_map.37 = f32[1024,256]{1,0:T(8,128)S(1)} custom-call(s32[2,2048]{1,0:T(2,128)S(1)} %bitcast.7, f32[2,512,128]{2,1,0:T(8,128)S(1)} %bitcast.6, f32[1024,256]{1,0:T(8,128)S(1)} %bitcast.5), custom_call_target="tpu_custom_call" | custom-call | tf_op jit(solution)/shard_map/pallas_call | solution.py:534
  58.0 1.2 %select_bitcast_fusion = f32[1,1024,256]{2,1,0:T(8,128)} fusion(f32[1024,256]{1,0:T(8,128)S(1)} %shard_map.37, pred[1024]{0:T(1024)(128)(4,1)S(1)} %fusion), kind=kLoop, calls=%fused_computation | loop fusion | flops 262144 | bytes 2098176 | tf_op jit(solution)/shard_map/broadcast_in_dim | solution.py:566
  (1 shorter events, 0.0 us)
Async XLA Ops:
  0.0 0.7 %copy-start.2 = (s32[1,2,2048]{2,1,0:T(2,128)S(1)}, s32[1,2,2048]{2,1,0:T(2,128)}, u32[]{:S(2)}) copy-start(s32[1,2,2048]{2,1,0:T(2,128)} %param.5) | copy-start | bytes 49156
  0.7 1.2 %copy-start = (f32[1,1024,256]{2,1,0:T(8,128)S(1)}, f32[1,1024,256]{2,1,0:T(8,128)}, u32[]{:S(2)}) copy-start(f32[1,1024,256]{2,1,0:T(8,128)} %param.3) | copy-start | bytes 3145732
  1.9 1.0 %copy-start.1 = (f32[1,2,512,128]{3,2,1,0:T(8,128)S(1)}, f32[1,2,512,128]{3,2,1,0:T(8,128)}, u32[]{:S(2)}) copy-start(f32[1,2,512,128]{3,2,1,0:T(8,128)} %param.4) | copy-start | bytes 1572868
